TPU v7x, 128 devices: a whole 4x4x4 slice. The times are simulated.
128 devices in a mesh: node: 16 (over y, z), chip: 8 (over x, core).
Axes of the slice: x: 4, y: 4, z: 4, core: 2. Of those that a mesh axis runs over, the one named last changes fastest.
Arguments:
- tokens: bfloat16 [32768, 2048], P(('node', 'chip')), may hold values from -6 to 6
- cotangent: bfloat16 [32768, 2048], P(('node', 'chip')), may hold values from -6 to 6
- chosen_rows: int32 [128, 256], P(('node', 'chip')), may hold values from 0 to 32767, as said below
- sensor_group: int32 [128], P(('node', 'chip')), may hold values from 0 to 3, as said below
- router: bfloat16 [128, 2048], P(('node', 'chip')), may hold values from -0.125 to 0.125
- gate_weight: bfloat16 [128, 2048, 1408], P(('node', 'chip')), may hold values from -0.125 to 0.125
- up_weight: bfloat16 [128, 2048, 1408], P(('node', 'chip')), may hold values from -0.125 to 0.125
- down_weight: bfloat16 [128, 1408, 2048], P(('node', 'chip')), may hold values from -0.15625 to 0.15625
Outputs:
- token_grad: bfloat16 [32768, 2048], P(('node', 'chip'))
- down_grad: bfloat16 [128, 1408, 2048], P(('node', 'chip'))
- router_grad: float32 [128, 2048], P(('node', 'chip'))
Inputs may be any that keep to these rules, and one draw needn't show every extreme that they name: `chosen_rows`: only the first 256 // 2**sensor_group[e] slots of expert e are live. The live picks of one expert are distinct rows, and at most 2 of them lie among the rows of one device (rows d * 256 to (d + 1) * 256 - 1); in every draw some expert takes exactly 2 rows from every device. For every device and every c, at most 8 of the experts e with e % 8 == c have live picks among that device's rows, and in every draw some device reaches 8. `sensor_group`: every sensor type names exactly 32 experts.
All inputs are finite; a program needn't handle non-finite values.
Results may differ from a plain program's by a relative error of at most 0.006.
Values may be sent and summed in bfloat16 or wider, within the bound.
A program may use at most 128 MiB of HBM per device.

v0:
```python
import jax
import jax.numpy as jnp
from jax import lax
from jax.sharding import PartitionSpec as P


def expert_backward(x_rows, dy_rows, router_row, w_gate, w_up, w_down):
    pre_gate = jnp.dot(x_rows, w_gate, preferred_element_type=jnp.float32)
    pre_up = jnp.dot(x_rows, w_up, preferred_element_type=jnp.float32)
    gate_sig = jax.nn.sigmoid(pre_gate)
    gate_act = pre_gate * gate_sig
    hidden = (gate_act * pre_up).astype(jnp.bfloat16)
    expert_out = jnp.dot(hidden, w_down, preferred_element_type=jnp.float32)
    score = jax.nn.sigmoid(jnp.dot(x_rows, router_row, preferred_element_type=jnp.float32))
    weight_grad = jnp.sum(dy_rows.astype(jnp.float32) * expert_out, axis=1)
    score_grad = weight_grad * score * (1.0 - score)
    out_grad = (score[:, None] * dy_rows.astype(jnp.float32)).astype(jnp.bfloat16)
    down_grad = jnp.dot(hidden.T, out_grad, preferred_element_type=jnp.float32).astype(jnp.bfloat16)
    hidden_grad = jnp.dot(out_grad, w_down.T, preferred_element_type=jnp.float32)
    gate_grad = (hidden_grad * pre_up * gate_sig * (1.0 + pre_gate * (1.0 - gate_sig))).astype(
        jnp.bfloat16
    )
    up_grad = (hidden_grad * gate_act).astype(jnp.bfloat16)
    pick_grad = jnp.dot(gate_grad, w_gate.T, preferred_element_type=jnp.float32)
    pick_grad = pick_grad + jnp.dot(up_grad, w_up.T, preferred_element_type=jnp.float32)
    pick_grad = pick_grad + score_grad[:, None] * router_row.astype(jnp.float32)[None, :]
    router_grad = jnp.dot(score_grad, x_rows.astype(jnp.float32), precision=lax.Precision.HIGHEST)
    return (pick_grad.astype(jnp.bfloat16), down_grad, router_grad)


def slot_fill(row_lists, live_count, first_row, row_count, per_source):
    capacity = row_lists.shape[-1]
    slot_index = jnp.arange(capacity, dtype=jnp.int32)
    local_row = row_lists - first_row
    mine = (slot_index < live_count[..., None]) & (local_row >= 0) & (local_row < row_count)
    rank_index = jnp.cumsum(mine.astype(jnp.int32), axis=-1) - 1
    placed = mine[..., None, :] & (
        rank_index[..., None, :] == jnp.arange(per_source, dtype=jnp.int32)[:, None]
    )
    slot_row = jnp.sum(jnp.where(placed, local_row[..., None, :], 0), axis=-1)
    filled = jnp.any(placed, axis=-1)
    return (slot_row, filled)


def local(
    tokens, cotangent, chosen_rows, sensor_group, router, gate_weight, up_weight, down_weight
):
    row_count, width = tokens.shape
    all_rows, all_groups = (
        lax.all_gather(chosen_rows, ("node", "chip"), axis=0, tiled=True),
        lax.all_gather(sensor_group, ("node", "chip"), axis=0, tiled=True),
    )
    expert_count, capacity = all_rows.shape
    per_source = capacity // expert_count
    my_index = lax.axis_index(("node", "chip"))
    live_count = jnp.right_shift(jnp.full((expert_count,), capacity, jnp.int32), all_groups)
    slot_row, filled = slot_fill(all_rows, live_count, my_index * row_count, row_count, per_source)
    selector = (
        slot_row[:, :, None] == jnp.arange(row_count, dtype=jnp.int32)[None, None, :]
    ) & filled[:, :, None]
    selector = selector.astype(jnp.bfloat16).reshape(expert_count * per_source, row_count)
    send_x = (
        jnp.dot(selector, tokens, preferred_element_type=jnp.float32)
        .astype(jnp.bfloat16)
        .reshape(expert_count, per_source, width)
    )
    send_dy = (
        jnp.dot(selector, cotangent, preferred_element_type=jnp.float32)
        .astype(jnp.bfloat16)
        .reshape(expert_count, per_source, width)
    )
    got_x, got_dy = (
        lax.all_to_all(send_x, ("node", "chip"), split_axis=0, concat_axis=0, tiled=True),
        lax.all_to_all(send_dy, ("node", "chip"), split_axis=0, concat_axis=0, tiled=True),
    )
    x_rows = got_x.reshape(-1, width)
    dy_rows = got_dy.reshape(-1, width)
    pick_grad, down_grad, router_grad = expert_backward(
        x_rows, dy_rows, router[0], gate_weight[0], up_weight[0], down_weight[0]
    )
    returned = lax.all_to_all(
        pick_grad.reshape(expert_count, per_source, width),
        ("node", "chip"),
        split_axis=0,
        concat_axis=0,
        tiled=True,
    )
    token_grad = lax.dot_general(
        selector,
        returned.reshape(-1, width),
        (((0,), (0,)), ((), ())),
        preferred_element_type=jnp.float32,
    )
    return (token_grad.astype(jnp.bfloat16), down_grad[None], router_grad[None])


def solution(mesh):
    return jax.shard_map(
        local,
        mesh=mesh,
        in_specs=(
            P(("node", "chip"), None),
            P(("node", "chip"), None),
            P(("node", "chip"), None),
            P(("node", "chip")),
            P(("node", "chip"), None),
            P(("node", "chip"), None, None),
            P(("node", "chip"), None, None),
            P(("node", "chip"), None, None),
        ),
        out_specs=(
            P(("node", "chip"), None),
            P(("node", "chip"), None, None),
            P(("node", "chip"), None),
        ),
        check_vma=False,
    )
```

profile of v0, /device:TPU:1, one launch (start us, length us, event | category | flops | bytes accessed | tf_op | source)
XLA Modules:
  0.0 205.2 jit_solution(11421926751713102351)
XLA Ops:
  0.6 0.0 copy-start
  1.4 0.1 dynamic-update-slice
  1.5 68.6 %all-reduce = s32[128]{0:T(128)S(1)} all-reduce(s32[128]{0:T(128)S(1)} %dynamic-update-slice), channel_id=1, replica_groups=mesh['node'=16,'chip'=8] {'node','chip'}, use_global_device_ids=true, to_apply=%add | all-reduce | flops 128 | bytes 1024
  70.2 33.6 %all-gather = s32[128,1,256]{2,1,0:T(1,128)S(1)} all-gather(s32[1,1,256]{2,1,0:T(1,128)} %bitcast.61), channel_id=1, replica_groups=mesh['node'=16,'chip'=8] {'node','chip'}, dimensions={0}, use_global_device_ids=true | all-gather | bytes 132096 | tf_op jit(solution)/shard_map/all_gather | solution.py:50
  103.8 0.1 copy.36
  103.9 0.1 fusion.41
  104.1 0.1 add_add_fusion
  104.2 0.1 copy.40
  104.3 0.1 copy.37
  104.4 0.1 fusion.34
  104.6 0.1 copy.43
  104.7 0.2 and.37
  104.9 0.1 copy.41
  105.0 0.1 select_reduce_fusion
  105.1 0.1 copy.42
  105.2 0.1 eq.41
  105.4 0.5 convolution_convert_fusion.2
  105.9 0.0 copy-start.2
  105.9 1.5 reshape.63
  107.4 4.8 %all-to-all-start = ((bf16[128,2,2048]{2,1,0:T(2,128)(2,1)}), bf16[128,2,2048]{2,1,0:T(2,128)(2,1)S(1)}, u32[]{:S(2)}, u32[]{:S(2)}) async-start(bf16[128,2,2048]{2,1,0:T(2,128)(2,1)} %reshape.63), calls=%async_computation | async-start | bytes 2097152 | tf_op jit(solution)/shard_map/all_to_all | solution.py:73
  112.3 1.7 convolution_convert_fusion.1
  114.0 1.5 reshape.65
  115.5 16.1 %all-to-all-done = bf16[128,2,2048]{2,1,0:T(2,128)(2,1)S(1)} async-done(((bf16[128,2,2048]{2,1,0:T(2,128)(2,1)}), bf16[128,2,2048]{2,1,0:T(2,128)(2,1)S(1)}, u32[]{:S(2)}, u32[]{:S(2)}) %all-to-all-start) | async-done | bytes 1048608 | tf_op jit(solution)/shard_map/all_to_all | solution.py:73
  131.6 1.0 copy-done.1
  132.5 4.3 %all-to-all-start.1 = ((bf16[128,2,2048]{2,1,0:T(2,128)(2,1)}), bf16[128,2,2048]{2,1,0:T(2,128)(2,1)S(1)}, u32[]{:S(2)}, u32[]{:S(2)}) async-start(bf16[128,2,2048]{2,1,0:T(2,128)(2,1)} %reshape.65), calls=%async_computation.1 | async-start | bytes 2097152 | tf_op jit(solution)/shard_map/all_to_all | solution.py:74
  136.9 1.5 reshape.64
  138.4 4.4 %fusion.3 = f32[256,1408]{1,0:T(8,128)S(1)} fusion(bf16[256,2048]{1,0:T(8,128)(2,1)S(1)} %reshape.64, bf16[1,2048,1408]{2,1,0:T(8,128)(2,1)} %param.13), kind=kOutput, calls=%fused_computation.4 | convolution fusion | flops 1476395008 | bytes 8257536 | tf_op jit(solution)/shard_map/dot_general | solution.py:8
  142.8 0.0 copy-start.3
  142.8 0.4 fusion.51
  143.2 0.7 copy-done.3
  143.9 5.8 %multiply_convert_fusion.2 = (bf16[256,1408]{1,0:T(8,128)(2,1)}, f32[256,1408]{1,0:T(8,128)}) fusion(f32[256,1408]{1,0:T(8,128)S(1)} %fusion.3, bf16[256,2048]{1,0:T(8,128)(2,1)S(1)} %reshape.64, bf16[1,2048,1408]{2,1,0:T(8,128)(2,1)} %param.14), kind=kOutput, calls=%fused_computation.24 | convolution fusion | flops 1478557696 | bytes 10420224 | tf_op jit(solution)/shard_map/dot_general | solution.py:9
  149.8 6.6 %all-to-all-done.1 = bf16[128,2,2048]{2,1,0:T(2,128)(2,1)S(1)} async-done(((bf16[128,2,2048]{2,1,0:T(2,128)(2,1)}), bf16[128,2,2048]{2,1,0:T(2,128)(2,1)S(1)}, u32[]{:S(2)}, u32[]{:S(2)}) %all-to-all-start.1) | async-done | bytes 1048608 | tf_op jit(solution)/shard_map/all_to_all | solution.py:74
  156.3 1.5 reshape.68
  157.8 5.4 %fusion.27 = f32[256]{0:T(256)S(1)} fusion(f32[256,2048]{1,0:T(8,128)} %reshape.68, bf16[256,1408]{1,0:T(8,128)(2,1)} %get-tuple-element.8, bf16[1,1408,2048]{2,1,0:T(8,128)(2,1)} %param.15), kind=kOutput, calls=%fused_computation.29 | convolution fusion | flops 1477443328 | bytes 8586240 | tf_op jit(solution)/shard_map/dot_general | solution.py:13
  163.2 0.1 mul.69
  163.4 1.9 multiply_convert_fusion.1
  165.2 1.5 convert_element_type.51
  166.7 0.0 slice-start
  166.7 4.6 %fusion.11 = f32[256,1408]{1,0:T(8,128)S(1)} fusion(bf16[256,2048]{1,0:T(8,128)(2,1)S(1)} %convert_element_type.51, bf16[1,1408,2048]{2,1,0:T(8,128)(2,1)} %param.15), kind=kOutput, calls=%fused_computation.12 | convolution fusion | flops 1476395008 | bytes 8257536 | tf_op jit(solution)/shard_map/dot_general | solution.py:19
  171.4 0.0 slice-start.1
  171.4 4.8 %fusion.1 = f32[256,2048]{1,0:T(8,128)S(1)} fusion(bf16[1,2048,1408]{2,1,0:T(8,128)(2,1)} %param.13, f32[256,1408]{1,0:T(8,128)S(1)} %copy-done.4, f32[256,1408]{1,0:T(8,128)S(1)} %fusion.11, f32[256,1408]{1,0:T(8,128)S(1)} %copy-done.5), kind=kOutput, calls=%fused_computation.2 | convolution fusion | flops 1479999488 | bytes 12189696 | tf_op jit(solution)/shard_map/dot_general | solution.py:24
  176.2 1.9 fusion.22
  178.1 1.5 reshape.66
  179.6 4.3 %all-to-all-start.2 = ((bf16[128,2,2048]{2,1,0:T(2,128)(2,1)}), bf16[128,2,2048]{2,1,0:T(2,128)(2,1)S(1)}, u32[]{:S(2)}, u32[]{:S(2)}) async-start(bf16[128,2,2048]{2,1,0:T(2,128)(2,1)} %reshape.66), calls=%async_computation.2 | async-start | bytes 2097152 | tf_op jit(solution)/shard_map/all_to_all | solution.py:81
  184.0 1.1 fusion.57
  185.1 6.1 %fusion = bf16[1,1408,2048]{2,1,0:T(8,128)(2,1)} fusion(bf16[256,1408]{1,0:T(8,128)(2,1)} %get-tuple-element.8, f32[256,2048]{1,0:T(8,128)} %reshape.68, f32[256]{0:T(256)S(1)} %get-tuple-element.4), kind=kOutput, calls=%fused_computation.1 | convolution fusion | flops 1480327168 | bytes 8586240 | tf_op jit(solution)/shard_map/dot_general | solution.py:18
  191.2 12.2 %all-to-all-done.2 = bf16[128,2,2048]{2,1,0:T(2,128)(2,1)S(1)} async-done(((bf16[128,2,2048]{2,1,0:T(2,128)(2,1)}), bf16[128,2,2048]{2,1,0:T(2,128)(2,1)S(1)}, u32[]{:S(2)}, u32[]{:S(2)}) %all-to-all-start.2) | async-done | bytes 1048608 | tf_op jit(solution)/shard_map/all_to_all | solution.py:81
  203.4 1.8 fusion.25
  (20 shorter events, 0.2 us)
Async XLA Ops:
  0.6 104.7 %copy-start = (bf16[256,2048]{1,0:T(8,128)(2,1)S(1)}, bf16[256,2048]{1,0:T(8,128)(2,1)}, u32[]{:S(2)}) copy-start(bf16[256,2048]{1,0:T(8,128)(2,1)} %param.8) | copy-start | bytes 3145732
  105.9 6.4 %copy-start.2 = (bf16[1,2048]{1,0:T(2,128)(2,1)S(1)}, bf16[1,2048]{1,0:T(2,128)(2,1)}, u32[]{:S(2)}) copy-start(bf16[1,2048]{1,0:T(2,128)(2,1)} %param.12) | copy-start | bytes 12292
  107.4 24.2 %all-to-all-start = ((bf16[128,2,2048]{2,1,0:T(2,128)(2,1)}), bf16[128,2,2048]{2,1,0:T(2,128)(2,1)S(1)}, u32[]{:S(2)}, u32[]{:S(2)}) async-start(bf16[128,2,2048]{2,1,0:T(2,128)(2,1)} %reshape.63), calls=%async_computation | async-start | bytes 2097152 | tf_op jit(solution)/shard_map/all_to_all | solution.py:73
  131.6 1.0 copy-start.1
  132.5 23.8 %all-to-all-start.1 = ((bf16[128,2,2048]{2,1,0:T(2,128)(2,1)}), bf16[128,2,2048]{2,1,0:T(2,128)(2,1)S(1)}, u32[]{:S(2)}, u32[]{:S(2)}) async-start(bf16[128,2,2048]{2,1,0:T(2,128)(2,1)} %reshape.65), calls=%async_computation.1 | async-start | bytes 2097152 | tf_op jit(solution)/shard_map/all_to_all | solution.py:74
  142.8 1.1 copy-start.3
  166.7 4.6 %copy-start.4 = (f32[256,1408]{1,0:T(8,128)S(1)}, f32[256,1408]{1,0:T(8,128)}, u32[]{:S(2)}) copy-start(f32[256,1408]{1,0:T(8,128)} %copy-done.3) | copy-start | bytes 4325380
  166.7 4.6 %copy-start.5 = (f32[256,1408]{1,0:T(8,128)S(1)}, f32[256,1408]{1,0:T(8,128)}, u32[]{:S(2)}) copy-start(f32[256,1408]{1,0:T(8,128)} %get-tuple-element.9) | copy-start | bytes 4325380
  166.7 9.5 %slice-start = ((s8[5767168]{0:T(1024)(128)(4,1)}), s8[4194304]{0:T(1024)(128)(4,1)S(1)}, s32[]{:S(2)}) async-start(s8[5767168]{0:T(1024)(128)(4,1)} %bitcast.62), calls=%async_computation.3 | async-start | bytes 8388608
  171.4 4.8 %slice-start.1 = ((s8[5767168]{0:T(1024)(128)(4,1)}), s8[1572864]{0:T(1024)(128)(4,1)S(1)}, s32[]{:S(2)}) async-start(s8[5767168]{0:T(1024)(128)(4,1)} %bitcast.62), calls=%async_computation.4 | async-start | bytes 3145728
  179.6 23.8 %all-to-all-start.2 = ((bf16[128,2,2048]{2,1,0:T(2,128)(2,1)}), bf16[128,2,2048]{2,1,0:T(2,128)(2,1)S(1)}, u32[]{:S(2)}, u32[]{:S(2)}) async-start(bf16[128,2,2048]{2,1,0:T(2,128)(2,1)} %reshape.66), calls=%async_computation.2 | async-start | bytes 2097152 | tf_op jit(solution)/shard_map/all_to_all | solution.py:81
where the time goes:
time: 206 us; the launch traced here: 205 us
  blocking collectives  102 us (50%)
  matrix products  38.6 us (19%)
  waiting for transfers between devices  34.8 us (17%)
  starting transfers between devices  13.5 us (7%)
  local copies, waits for them, and re-layouts  11.9 us (6%)
  other arithmetic  2.45 us (1%)
    unnamed x1, blocking collectives  68.6 us
    all_gather x1, blocking collectives, local(): lax.all_gather(chosen_rows, ('node', 'chip'), axis=0, tiled=True)  33.6 us
    all_to_all x1, waiting for transfers between devices, local(): lax.all_to_all(send_x, ('node', 'chip'), split_axis=0, concat_axis=0, til...  16.1 us
    all_to_all x1, waiting for transfers between devices, local(): lax.all_to_all(pick_grad.reshape(expert_count, per_source, width), ('node...  12.2 us
    all_to_all x1, waiting for transfers between devices, local(): lax.all_to_all(send_dy, ('node', 'chip'), split_axis=0, concat_axis=0, ti...  6.58 us
    dot_general x1, matrix products, expert_backward(): jnp.dot(hidden.T, out_grad, preferred_element_type=jnp.float32)  6.1 us
    dot_general x1, matrix products, expert_backward(): pre_up = jnp.dot(x_rows, w_up, preferred_element_type=jnp.float32)  5.84 us
    dot_general x1, matrix products, expert_backward(): expert_out = jnp.dot(hidden, w_down, preferred_element_type=jnp.float32)  5.37 us
  transfers between devices with their start and end apart: 3, of which 3 were waited for; matrix products, arithmetic and copies ran while one was open for 11% of the time, Pallas kernels for 0%

commit v1 on v0

v1 whole, which is shorter than its diff:
```python
import functools

import jax
import jax.numpy as jnp
from jax import lax
from jax.experimental import pallas as pl
from jax.experimental.pallas import tpu as pltpu
from jax.sharding import PartitionSpec as P

MESH = pl.DeviceIdType.MESH
F32 = jnp.float32
BF16 = jnp.bfloat16
BLOCK = 16
STEPS = 4


def dot(a, b):
    return jnp.dot(a, b, preferred_element_type=F32)


def dot_nt(a, b):
    return lax.dot_general(a, b, (((1,), (1,)), ((), ())), preferred_element_type=F32)


def exchange_kernel(
    n_node,
    n_chip,
    chosen,
    group,
    router,
    tokens,
    cotangent,
    w_gate_hbm,
    w_up_hbm,
    w_down_hbm,
    ret_out,
    scatter_out,
    hidden_t_out,
    out_grad_out,
    router_grad,
    both,
    w_gate,
    w_up,
    w_down,
    list_send,
    lists,
    expand,
    compact,
    pick_send,
    pick_mine,
    stage_a,
    mid,
    stage_b,
    rows,
    pre_gate,
    pre_up,
    raw,
    score,
    hidden,
    hidden_t,
    gate_grad,
    up_grad,
    score_grad,
    out_grad,
    back,
    back_mid,
    back_stage,
    ret,
    scatter,
    load_sem,
    store_sem,
    list_sem,
    pick_sem,
    a_send,
    a_recv,
    b_send,
    b_recv,
    rb_send,
    rb_recv,
    ra_send,
    ra_recv,
):
    n = lax.axis_index("node")
    c = lax.axis_index("chip")
    width = router.shape[1]
    ff = w_gate.shape[1]
    chunk = width // STEPS
    dense = n_node * BLOCK
    packed = n_chip * BLOCK

    loads = [
        pltpu.make_async_copy(tokens, both.at[:, pl.ds(0, width)], load_sem.at[0]),
        pltpu.make_async_copy(cotangent, both.at[:, pl.ds(width, width)], load_sem.at[1]),
        pltpu.make_async_copy(w_gate_hbm, w_gate, load_sem.at[2]),
        pltpu.make_async_copy(w_up_hbm, w_up, load_sem.at[3]),
        pltpu.make_async_copy(w_down_hbm, w_down, load_sem.at[4]),
    ]
    for load in loads:
        load.start()

    def node_peer(i):
        return lax.rem(n + i, n_node)

    def chip_peer(i):
        return lax.rem(c + i, n_chip)

    barrier = pltpu.get_barrier_semaphore()

    def greet_node(i, carry):
        pl.semaphore_signal(barrier, inc=1, device_id=(node_peer(i), c), device_id_type=MESH)
        return carry

    def greet_chip(i, carry):
        pl.semaphore_signal(barrier, inc=1, device_id=(n, chip_peer(i)), device_id_type=MESH)
        return carry

    lax.fori_loop(1, n_node, greet_node, 0)
    lax.fori_loop(1, n_chip, greet_chip, 0)

    cap = chosen.shape[1]
    slot_index = lax.broadcasted_iota(jnp.int32, (8, cap), 1)
    live = jnp.right_shift(jnp.full((8, cap), cap, jnp.int32), jnp.broadcast_to(group[...], (8, cap)))
    own_list = jnp.where(slot_index < live, jnp.broadcast_to(chosen[...], (8, cap)), -1)
    list_send[...] = own_list
    lists[pl.ds(pl.multiple_of(n * 8, 8), 8), :] = own_list

    pl.semaphore_wait(barrier, n_node + n_chip - 2)

    def send_list(i, carry):
        pltpu.make_async_remote_copy(
            src_ref=list_send,
            dst_ref=lists.at[pl.ds(pl.multiple_of(n * 8, 8), 8), :],
            send_sem=list_sem.at[0],
            recv_sem=list_sem.at[1],
            device_id=(node_peer(i), c),
            device_id_type=MESH,
        ).start()
        return carry

    lax.fori_loop(1, n_node, send_list, 0)

    pre_gate[...] = jnp.zeros_like(pre_gate)
    pre_up[...] = jnp.zeros_like(pre_up)
    raw[...] = jnp.zeros_like(raw)
    score[...] = jnp.zeros_like(score)

    def wait_bytes(ref, sem):
        pltpu.make_async_copy(ref, ref, sem).wait()

    wait_bytes(lists.at[pl.ds(0, (n_node - 1) * 8), :], list_sem.at[0])
    wait_bytes(lists.at[pl.ds(0, (n_node - 1) * 8), :], list_sem.at[1])

    source = lax.broadcasted_iota(jnp.int32, (8, 1), 0)
    lane_row = lax.broadcasted_iota(jnp.int32, (8, cap), 1)
    lane_slot = lax.broadcasted_iota(jnp.int32, (8, packed), 1)
    used = jnp.zeros((8, 1), jnp.int32)
    expand_parts, row_parts = [], []
    for e in range(n_node):
        listed = lists[8 * e : 8 * e + 8, :]
        mine = jnp.right_shift(listed, 8) == n * n_chip + source
        local_row = jnp.bitwise_and(listed, 255)
        low = jnp.min(jnp.where(mine, local_row, 256), axis=1, keepdims=True)
        high = jnp.max(jnp.where(mine, local_row, -1), axis=1, keepdims=True)
        place = source * BLOCK + used
        first = jnp.where(high >= 0, place, -1)
        second = jnp.where(high > low, place + 8, -1)
        expand_parts.append(jnp.where(lane_slot == first, 1.0, 0.0))
        expand_parts.append(jnp.where(lane_slot == second, 1.0, 0.0))
        row_parts.append(jnp.where(lane_row == low, 1.0, 0.0))
        row_parts.append(jnp.where(lane_row == high, 1.0, 0.0))
        used = used + jnp.where(high >= 0, 1, 0)
    expand_f32 = jnp.concatenate(expand_parts, axis=0)
    expand[...] = expand_f32.astype(BF16)
    compact[...] = expand_f32.T.astype(BF16)
    row_hot = jnp.concatenate(row_parts, axis=0).astype(BF16)
    pick_send[...] = dot(compact[...], row_hot).astype(BF16)

    def block(i):
        return pl.ds(pl.multiple_of(i * BLOCK, BLOCK), BLOCK)

    def send_pick(i, carry):
        to = chip_peer(i)
        pltpu.make_async_remote_copy(
            src_ref=pick_send.at[block(to), :],
            dst_ref=pick_mine.at[block(c), :],
            send_sem=pick_sem.at[0],
            recv_sem=pick_sem.at[1],
            device_id=(n, to),
            device_id_type=MESH,
        ).start()
        return carry

    lax.fori_loop(1, n_chip, send_pick, 0)
    pick_mine[block(c), :] = pick_send[block(c), :]
    loads[0].wait()
    loads[1].wait()
    wait_bytes(pick_mine.at[pl.ds(0, (n_chip - 1) * BLOCK), :], pick_sem.at[0])
    wait_bytes(pick_mine.at[pl.ds(0, (n_chip - 1) * BLOCK), :], pick_sem.at[1])

    def cols(s):
        return pl.ds(pl.multiple_of(s * chunk, chunk), chunk)

    def to_chips(src, dst, s, send_sem, recv_sem):
        def one(i, carry):
            to = chip_peer(i)
            pltpu.make_async_remote_copy(
                src_ref=src.at[block(to), cols(s)],
                dst_ref=dst.at[block(c), cols(s)],
                send_sem=send_sem.at[s],
                recv_sem=recv_sem.at[s],
                device_id=(n, to),
                device_id_type=MESH,
            ).start()
            return carry

        lax.fori_loop(1, n_chip, one, 0)
        dst[block(c), cols(s)] = src[block(c), cols(s)]

    def to_nodes(src, dst, s, send_sem, recv_sem):
        def one(i, carry):
            to = node_peer(i)
            pltpu.make_async_remote_copy(
                src_ref=src.at[block(to), cols(s)],
                dst_ref=dst.at[block(n), cols(s)],
                send_sem=send_sem.at[s],
                recv_sem=recv_sem.at[s],
                device_id=(to, c),
                device_id_type=MESH,
            ).start()
            return carry

        lax.fori_loop(1, n_node, one, 0)
        dst[block(n), cols(s)] = src[block(n), cols(s)]

    def chips_done(ref, s, sem):
        wait_bytes(ref.at[pl.ds(0, packed - BLOCK), cols(s)], sem.at[s])

    def nodes_done(ref, s, sem):
        wait_bytes(ref.at[pl.ds(0, dense - BLOCK), cols(s)], sem.at[s])

    def gather(s):
        stage_a[:, cols(s)] = dot(pick_mine[...], both[:, cols(s)]).astype(BF16)
        to_chips(stage_a, mid, s, a_send, a_recv)

    def forward(s):
        chips_done(mid, s, a_recv)
        stage_b[:, cols(s)] = dot(expand[...], mid[:, cols(s)]).astype(BF16)
        to_nodes(stage_b, rows, s, b_send, b_recv)

    def up_step(s):
        nodes_done(rows, s, b_recv)
        x = rows[:, cols(s)]
        pre_gate[...] += dot(x, w_gate[cols(s), :])
        pre_up[...] += dot(x, w_up[cols(s), :])
        score[...] += dot_nt(x, jnp.broadcast_to(router[:, cols(s)], (128, chunk)))

    def down_step(s):
        nodes_done(rows, s, b_recv)
        raw[...] += dot_nt(rows[:, cols(s)], w_down[:, cols(s - STEPS)])

    gather(0)
    scatter[...] = pick_mine[...].astype(F32).T.astype(BF16)
    scatter_store = pltpu.make_async_copy(scatter, scatter_out, store_sem.at[0])
    scatter_store.start()
    gather(1)
    forward(0)
    loads[2].wait()
    loads[3].wait()

    def x_phase(s, carry):
        gather(s + 1)
        forward(s)
        up_step(s - 1)
        return carry

    lax.fori_loop(1, STEPS + 1, x_phase, 0)

    def from_x(r, carry):
        part = pl.ds(pl.multiple_of(r * 64, 64), 64)
        s = jax.nn.sigmoid(score[part, :])
        score[part, :] = s
        for j in range(ff // 128):
            lanes = pl.ds(128 * j, 128)
            g = pre_gate[part, lanes]
            u = pre_up[part, lanes]
            sig = jax.nn.sigmoid(g)
            act = g * sig
            hidden[part, lanes] = (act * u).astype(BF16)
            pre_gate[part, lanes] = s * (u * sig * (1.0 + g * (1.0 - sig)))
            pre_up[part, lanes] = s * act
        return carry

    lax.fori_loop(0, dense // 64, from_x, 0)
    loads[4].wait()

    def dy_phase(s, carry):
        @pl.when(s + 1 < 2 * STEPS)
        def _():
            gather(s + 1)

        forward(s)
        down_step(s - 1)
        return carry

    lax.fori_loop(STEPS + 1, 2 * STEPS, dy_phase, 0)
    down_step(2 * STEPS - 1)

    def from_dy(r, carry):
        part = pl.ds(pl.multiple_of(r * 64, 64), 64)
        total = jnp.zeros((64, 128), F32)
        for j in range(ff // 128):
            lanes = pl.ds(128 * j, 128)
            v = raw[part, lanes]
            total = total + v * hidden[part, lanes].astype(F32)
            gate_grad[part, lanes] = (v * pre_gate[part, lanes]).astype(BF16)
            up_grad[part, lanes] = (v * pre_up[part, lanes]).astype(BF16)
        s = score[part, :]
        score_grad[part, :] = jnp.sum(total, axis=1, keepdims=True) * s * (1.0 - s)
        return carry

    lax.fori_loop(0, dense // 64, from_dy, 0)

    def send_back(s):
        value = dot_nt(gate_grad[...], w_gate[cols(s), :])
        value = value + dot_nt(up_grad[...], w_up[cols(s), :])
        value = value + score_grad[:, :1] * router[:, cols(s)].astype(F32)
        back[:, cols(s)] = value.astype(BF16)
        to_nodes(back, back_mid, s, rb_send, rb_recv)

    def send_home(s):
        nodes_done(back_mid, s, rb_recv)
        back_stage[:, cols(s)] = dot(compact[...], back_mid[:, cols(s)]).astype(BF16)
        to_chips(back_stage, ret, s, ra_send, ra_recv)

    send_back(0)
    hidden_t[...] = hidden[...].astype(F32).T.astype(BF16)
    hidden_store = pltpu.make_async_copy(hidden_t, hidden_t_out, store_sem.at[1])
    hidden_store.start()

    def return_phase(s, carry):
        send_back(s)
        send_home(s - 1)
        return carry

    lax.fori_loop(1, STEPS, return_phase, 0)

    def scale(r, carry):
        part = pl.ds(pl.multiple_of(r * 16, 16), 16)
        s = score[part, :1]
        out_grad[part, :] = (s * rows[part, width:].astype(F32)).astype(BF16)
        return carry

    lax.fori_loop(0, dense // 16, scale, 0)
    grad_store = pltpu.make_async_copy(out_grad, out_grad_out, store_sem.at[2])
    grad_store.start()

    across = score_grad[...].T[:16, :]
    part0 = across.astype(BF16)
    rest = across - part0.astype(F32)
    part1 = rest.astype(BF16)
    part2 = (rest - part1.astype(F32)).astype(BF16)
    for s in range(STEPS):
        x = rows[:, s * chunk : (s + 1) * chunk]
        value = dot(part0, x) + (dot(part1, x) + dot(part2, x))
        router_grad[:, s * chunk : (s + 1) * chunk] = value[:1, :]

    send_home(STEPS - 1)

    def home(s, carry):
        chips_done(ret, s, ra_recv)
        return carry

    lax.fori_loop(0, STEPS, home, 0)
    ret_store = pltpu.make_async_copy(ret, ret_out, store_sem.at[3])
    ret_store.start()

    def drain_out(s, carry):
        chips_done(stage_a, s, a_send)
        nodes_done(stage_b, s, b_send)
        return carry

    def drain_back(s, carry):
        nodes_done(back, s, rb_send)
        chips_done(back_stage, s, ra_send)
        return carry

    lax.fori_loop(0, 2 * STEPS, drain_out, 0)
    lax.fori_loop(0, STEPS, drain_back, 0)
    scatter_store.wait()
    hidden_store.wait()
    grad_store.wait()
    ret_store.wait()


def finish_kernel(scatter, ret, hidden_t, out_grad, token_grad, down_grad, token_buf, down_buf, sem):
    ff = hidden_t.shape[0]
    step = 128

    def one(i, carry):
        part = pl.ds(pl.multiple_of(i * step, step), step)
        down_buf[part, :] = dot(hidden_t[part, :], out_grad[...]).astype(BF16)
        pltpu.make_async_copy(down_buf.at[part, :], down_grad.at[part, :], sem.at[0]).start()
        return carry

    lax.fori_loop(0, ff // step, one, 0)
    token_buf[...] = dot(scatter[...], ret[...]).astype(BF16)
    store = pltpu.make_async_copy(token_buf, token_grad, sem.at[1])
    store.start()
    pltpu.make_async_copy(down_buf, down_grad, sem.at[0]).wait()
    store.wait()


def local(n_node, n_chip, tokens, cotangent, chosen, group, router, w_gate, w_up, w_down):
    row_count, width = tokens.shape
    ff = w_gate.shape[2]
    cap = chosen.shape[1]
    dense = n_node * BLOCK
    packed = n_chip * BLOCK
    vmem = pl.BlockSpec(memory_space=pltpu.VMEM)
    hbm = pl.BlockSpec(memory_space=pl.ANY)
    dma = pltpu.SemaphoreType.DMA
    ret, scatter, hidden_t, out_grad, router_grad = pl.pallas_call(
        functools.partial(exchange_kernel, n_node, n_chip),
        out_shape=[
            jax.ShapeDtypeStruct((packed, width), BF16),
            jax.ShapeDtypeStruct((row_count, packed), BF16),
            jax.ShapeDtypeStruct((ff, dense), BF16),
            jax.ShapeDtypeStruct((dense, width), BF16),
            jax.ShapeDtypeStruct((1, width), F32),
        ],
        in_specs=[vmem] * 3 + [hbm] * 5,
        out_specs=[hbm] * 4 + [vmem],
        scratch_shapes=[
            pltpu.VMEM((row_count, 2 * width), BF16),
            pltpu.VMEM((width, ff), BF16),
            pltpu.VMEM((width, ff), BF16),
            pltpu.VMEM((ff, width), BF16),
            pltpu.VMEM((8, cap), jnp.int32),
            pltpu.VMEM((8 * n_node, cap), jnp.int32),
            pltpu.VMEM((dense, packed), BF16),
            pltpu.VMEM((packed, dense), BF16),
            pltpu.VMEM((packed, row_count), BF16),
            pltpu.VMEM((packed, row_count), BF16),
            pltpu.VMEM((packed, 2 * width), BF16),
            pltpu.VMEM((packed, 2 * width), BF16),
            pltpu.VMEM((dense, 2 * width), BF16),
            pltpu.VMEM((dense, 2 * width), BF16),
            pltpu.VMEM((dense, ff), F32),
            pltpu.VMEM((dense, ff), F32),
            pltpu.VMEM((dense, ff), F32),
            pltpu.VMEM((dense, 128), F32),
            pltpu.VMEM((dense, ff), BF16),
            pltpu.VMEM((ff, dense), BF16),
            pltpu.VMEM((dense, ff), BF16),
            pltpu.VMEM((dense, ff), BF16),
            pltpu.VMEM((dense, 128), F32),
            pltpu.VMEM((dense, width), BF16),
            pltpu.VMEM((dense, width), BF16),
            pltpu.VMEM((dense, width), BF16),
            pltpu.VMEM((packed, width), BF16),
            pltpu.VMEM((packed, width), BF16),
            pltpu.VMEM((row_count, packed), BF16),
            dma((5,)),
            dma((4,)),
            dma((2,)),
            dma((2,)),
            dma((2 * STEPS,)),
            dma((2 * STEPS,)),
            dma((2 * STEPS,)),
            dma((2 * STEPS,)),
            dma((STEPS,)),
            dma((STEPS,)),
            dma((STEPS,)),
            dma((STEPS,)),
        ],
        compiler_params=pltpu.CompilerParams(
            collective_id=0, has_side_effects=True, vmem_limit_bytes=56 * 1024 * 1024
        ),
        name="exchange",
    )(
        chosen,
        group.reshape(1, 1),
        router,
        tokens,
        cotangent,
        w_gate[0],
        w_up[0],
        w_down[0],
    )
    token_grad, down_grad = pl.pallas_call(
        finish_kernel,
        out_shape=[
            jax.ShapeDtypeStruct((row_count, width), BF16),
            jax.ShapeDtypeStruct((ff, width), BF16),
        ],
        in_specs=[vmem] * 4,
        out_specs=[hbm] * 2,
        scratch_shapes=[
            pltpu.VMEM((row_count, width), BF16),
            pltpu.VMEM((ff, width), BF16),
            dma((2,)),
        ],
        compiler_params=pltpu.CompilerParams(vmem_limit_bytes=32 * 1024 * 1024),
        name="finish",
    )(scatter, ret, hidden_t, out_grad)
    return token_grad, down_grad[None], router_grad


def solution(mesh):
    rows = P(("node", "chip"), None)
    weight = P(("node", "chip"), None, None)
    return jax.shard_map(
        functools.partial(local, mesh.shape["node"], mesh.shape["chip"]),
        mesh=mesh,
        in_specs=(rows, rows, rows, P(("node", "chip")), rows, weight, weight, weight),
        out_specs=(rows, weight, rows),
        check_vma=False,
    )
```

time: 206 us -> 98 us (0.48)
  blocking collectives: 102 us -> 0 us
  Pallas kernels: 0 us -> 90.8 us
  matrix products: 38.6 us -> 0 us
  waiting for transfers between devices: 34.8 us -> 0 us
  starting transfers between devices: 13.5 us -> 0 us
  local copies, waits for them, and re-layouts: 11.9 us -> 5.5 us
  other arithmetic: 2.45 us -> 0 us
    pallas_call x0 -> x2, Pallas kernels: none -> 90.8 us  [the longest x1 86 us: local(): pl.pallas_call(functools.partial(exchange_kernel, n_node, n_chip), out_sh...]
    unnamed x1 -> x0, blocking collectives: 68.6 us -> none
    dot_general x12 -> x0, matrix products: 38.6 us -> none  [the longest x1 6.1 us: expert_backward(): jnp.dot(hidden.T, out_grad, preferred_element_type=jnp.float32)]
    all_to_all x3 -> x0, waiting for transfers between devices: 34.8 us -> none  [the longest x1 16.1 us: local(): lax.all_to_all(send_x, ('node', 'chip'), split_axis=0, concat_axis=0, til...]
    all_gather x1 -> x0, blocking collectives: 33.6 us -> none  [local(): lax.all_gather(chosen_rows, ('node', 'chip'), axis=0, tiled=True)]
    all_to_all x3 -> x0, starting transfers between devices: 13.5 us -> none  [the longest x1 4.85 us: local(): lax.all_to_all(send_x, ('node', 'chip'), split_axis=0, concat_axis=0, til...]
    reshape x4 -> x0, local copies, waits for them, and re-layouts: 5.99 us -> none  [the longest x1 1.52 us: local(): send_dy = jnp.dot(selector, cotangent, preferred_element_type=jnp.float32...]
    unnamed x18 -> x9, local copies, waits for them, and re-layouts: 1.85 us -> 5.5 us
  transfers between devices with their start and end apart: 3 -> 0, of which waited for: 3 -> 0; matrix products, arithmetic and copies ran while one was open for 11% -> 0% of each run, Pallas kernels for 0% -> 0%
where the time goes in v1:
time: 98 us; the launch traced here: 97.6 us
  Pallas kernels  90.8 us (93%)
  local copies, waits for them, and re-layouts  5.5 us (6%)
  between operations  1.31 us (1%)
    pallas_call x1, Pallas kernels, local(): pl.pallas_call(functools.partial(exchange_kernel, n_node, n_chip), out_sh...  86 us
    unnamed x9, local copies, waits for them, and re-layouts  5.5 us
    pallas_call x1, Pallas kernels, local(): pl.pallas_call(finish_kernel, out_shape=[jax.ShapeDtypeStruct((row_count,...  4.87 us

profile of v1, /device:TPU:1, one launch (start us, length us, event | category | flops | bytes accessed | tf_op | source)
XLA Modules:
  0.0 97.6 jit_solution(11611062563617596926)
XLA Ops:
  1.3 86.0 %exchange.1 = (bf16[128,2048]{1,0:T(8,128)(2,1)}, bf16[256,128]{1,0:T(8,128)(2,1)}, bf16[1408,256]{1,0:T(8,128)(2,1)}, bf16[256,2048]{1,0:T(8,128)(2,1)}, f32[1,2048]{1,0:T(1,128)}) custom-call(s32[1,256]{1,0:T(1,128)} %chosen.1, s32[1,1]{1,0:T(1,128)} %bitcast.5.group, bf16[1,2048]{1,0:T(2,128)(2,1)} %router.1, bf16[256,2048]{1,0:T(8,128)(2,1)} %tokens.1, ...), custom_call_target="tpu_custom_call" | custom-call | tf_op jit(solution)/shard_map/exchange/pallas_call | solution.py:422
  87.2 0.0 copy-start
  87.3 1.2 %copy-done = bf16[256,2048]{1,0:T(8,128)(2,1)S(1)} copy-done((bf16[256,2048]{1,0:T(8,128)(2,1)S(1)}, bf16[256,2048]{1,0:T(8,128)(2,1)}, u32[]{:S(2)}) %copy-start) | copy-done | bytes 1048600
  88.5 0.0 copy-start.1
  88.5 1.1 %copy-done.1 = bf16[1408,256]{1,0:T(8,128)(2,1)S(1)} copy-done((bf16[1408,256]{1,0:T(8,128)(2,1)S(1)}, bf16[1408,256]{1,0:T(8,128)(2,1)}, u32[]{:S(2)}) %copy-start.1) | copy-done | bytes 720920
  89.6 0.0 copy-start.2
  89.6 1.0 %copy-done.2 = bf16[128,2048]{1,0:T(8,128)(2,1)S(1)} copy-done((bf16[128,2048]{1,0:T(8,128)(2,1)S(1)}, bf16[128,2048]{1,0:T(8,128)(2,1)}, u32[]{:S(2)}) %copy-start.2) | copy-done | bytes 524312
  90.6 0.0 copy-start.3
  90.6 0.8 copy-done.3
  91.5 4.9 %finish.1 = (bf16[256,2048]{1,0:T(8,128)(2,1)}, bf16[1408,2048]{1,0:T(8,128)(2,1)}) custom-call(bf16[256,128]{1,0:T(8,128)(2,1)S(1)} %copy-done.3, bf16[128,2048]{1,0:T(8,128)(2,1)S(1)} %copy-done.2, bf16[1408,256]{1,0:T(8,128)(2,1)S(1)} %copy-done.1, bf16[256,2048]{1,0:T(8,128)(2,1)S(1)} %copy-done), custom_call_target="tpu_custom_call" | custom-call | tf_op jit(solution)/shard_map/finish/pallas_call | solution.py:490
  96.3 1.3 %copy.13 = f32[1,2048]{1,0:T(1,128)} copy(f32[1,2048]{1,0:T(1,128)} %get-tuple-element.22) | data formatting | bytes 16384
Async XLA Ops:
  87.2 1.2 %copy-start = (bf16[256,2048]{1,0:T(8,128)(2,1)S(1)}, bf16[256,2048]{1,0:T(8,128)(2,1)}, u32[]{:S(2)}) copy-start(bf16[256,2048]{1,0:T(8,128)(2,1)} %get-tuple-element.13.out_grad) | copy-start | bytes 3145732
  88.5 1.1 %copy-start.1 = (bf16[1408,256]{1,0:T(8,128)(2,1)S(1)}, bf16[1408,256]{1,0:T(8,128)(2,1)}, u32[]{:S(2)}) copy-start(bf16[1408,256]{1,0:T(8,128)(2,1)} %get-tuple-element.12.hidden_t) | copy-start | bytes 2162692
  89.6 1.0 %copy-start.2 = (bf16[128,2048]{1,0:T(8,128)(2,1)S(1)}, bf16[128,2048]{1,0:T(8,128)(2,1)}, u32[]{:S(2)}) copy-start(bf16[128,2048]{1,0:T(8,128)(2,1)} %get-tuple-element.11.ret) | copy-start | bytes 1572868
  90.6 0.8 copy-start.3

commit v2 on v1

--- a/solution.py
+++ b/solution.py
@@ -12,6 +12,8 @@
 BF16 = jnp.bfloat16
 BLOCK = 16
 STEPS = 4
+LEAD = 2
+LAG = 3
 
 
 def dot(a, b):
@@ -25,9 +27,9 @@
 def exchange_kernel(
     n_node,
     n_chip,
-    chosen,
+    chosen_hbm,
     group,
-    router,
+    router_hbm,
     tokens,
     cotangent,
     w_gate_hbm,
@@ -37,7 +39,9 @@
     scatter_out,
     hidden_t_out,
     out_grad_out,
-    router_grad,
+    router_grad_out,
+    chosen,
+    router,
     both,
     w_gate,
     w_up,
@@ -67,6 +71,7 @@
     back_stage,
     ret,
     scatter,
+    router_grad,
     load_sem,
     store_sem,
     list_sem,
@@ -88,6 +93,12 @@
     dense = n_node * BLOCK
     packed = n_chip * BLOCK
 
+    small_loads = [
+        pltpu.make_async_copy(chosen_hbm, chosen, load_sem.at[5]),
+        pltpu.make_async_copy(router_hbm, router, load_sem.at[6]),
+    ]
+    for load in small_loads:
+        load.start()
     loads = [
         pltpu.make_async_copy(tokens, both.at[:, pl.ds(0, width)], load_sem.at[0]),
         pltpu.make_async_copy(cotangent, both.at[:, pl.ds(width, width)], load_sem.at[1]),
@@ -117,6 +128,8 @@
     lax.fori_loop(1, n_node, greet_node, 0)
     lax.fori_loop(1, n_chip, greet_chip, 0)
 
+    for load in small_loads:
+        load.wait()
     cap = chosen.shape[1]
     slot_index = lax.broadcasted_iota(jnp.int32, (8, cap), 1)
     live = jnp.right_shift(jnp.full((8, cap), cap, jnp.int32), jnp.broadcast_to(group[...], (8, cap)))
@@ -258,23 +271,6 @@
         nodes_done(rows, s, b_recv)
         raw[...] += dot_nt(rows[:, cols(s)], w_down[:, cols(s - STEPS)])
 
-    gather(0)
-    scatter[...] = pick_mine[...].astype(F32).T.astype(BF16)
-    scatter_store = pltpu.make_async_copy(scatter, scatter_out, store_sem.at[0])
-    scatter_store.start()
-    gather(1)
-    forward(0)
-    loads[2].wait()
-    loads[3].wait()
-
-    def x_phase(s, carry):
-        gather(s + 1)
-        forward(s)
-        up_step(s - 1)
-        return carry
-
-    lax.fori_loop(1, STEPS + 1, x_phase, 0)
-
     def from_x(r, carry):
         part = pl.ds(pl.multiple_of(r * 64, 64), 64)
         s = jax.nn.sigmoid(score[part, :])
@@ -290,20 +286,42 @@
             pre_up[part, lanes] = s * act
         return carry
 
-    lax.fori_loop(0, dense // 64, from_x, 0)
-    loads[4].wait()
-
-    def dy_phase(s, carry):
-        @pl.when(s + 1 < 2 * STEPS)
+    for s in range(LEAD):
+        gather(s)
+    scatter[...] = pick_mine[...].astype(F32).T.astype(BF16)
+    scatter_store = pltpu.make_async_copy(scatter, scatter_out, store_sem.at[0])
+    scatter_store.start()
+
+    def phase(t, carry):
+        @pl.when(t + LEAD < 2 * STEPS)
         def _():
-            gather(s + 1)
-
-        forward(s)
-        down_step(s - 1)
-        return carry
-
-    lax.fori_loop(STEPS + 1, 2 * STEPS, dy_phase, 0)
-    down_step(2 * STEPS - 1)
+            gather(t + LEAD)
+
+        @pl.when(t < 2 * STEPS)
+        def _():
+            forward(t)
+
+        @pl.when(t == LAG)
+        def _():
+            loads[2].wait()
+            loads[3].wait()
+
+        @pl.when((t >= LAG) & (t < STEPS + LAG))
+        def _():
+            up_step(t - LAG)
+
+        @pl.when(t == STEPS + LAG)
+        def _():
+            lax.fori_loop(0, dense // 64, from_x, 0)
+            loads[4].wait()
+
+        @pl.when(t >= STEPS + LAG)
+        def _():
+            down_step(t - LAG)
+
+        return carry
+
+    lax.fori_loop(0, 2 * STEPS + LAG, phase, 0)
 
     def from_dy(r, carry):
         part = pl.ds(pl.multiple_of(r * 64, 64), 64)
@@ -332,17 +350,14 @@
         back_stage[:, cols(s)] = dot(compact[...], back_mid[:, cols(s)]).astype(BF16)
         to_chips(back_stage, ret, s, ra_send, ra_recv)
 
-    send_back(0)
+    def return_phase(s, carry):
+        send_back(s)
+        return carry
+
+    lax.fori_loop(0, STEPS, return_phase, 0)
     hidden_t[...] = hidden[...].astype(F32).T.astype(BF16)
     hidden_store = pltpu.make_async_copy(hidden_t, hidden_t_out, store_sem.at[1])
     hidden_store.start()
-
-    def return_phase(s, carry):
-        send_back(s)
-        send_home(s - 1)
-        return carry
-
-    lax.fori_loop(1, STEPS, return_phase, 0)
 
     def scale(r, carry):
         part = pl.ds(pl.multiple_of(r * 16, 16), 16)
@@ -364,7 +379,14 @@
         value = dot(part0, x) + (dot(part1, x) + dot(part2, x))
         router_grad[:, s * chunk : (s + 1) * chunk] = value[:1, :]
 
-    send_home(STEPS - 1)
+    router_store = pltpu.make_async_copy(router_grad, router_grad_out, store_sem.at[4])
+    router_store.start()
+
+    def home_phase(s, carry):
+        send_home(s)
+        return carry
+
+    lax.fori_loop(0, STEPS, home_phase, 0)
 
     def home(s, carry):
         chips_done(ret, s, ra_recv)
@@ -389,25 +411,59 @@
     scatter_store.wait()
     hidden_store.wait()
     grad_store.wait()
+    router_store.wait()
     ret_store.wait()
 
 
-def finish_kernel(scatter, ret, hidden_t, out_grad, token_grad, down_grad, token_buf, down_buf, sem):
+def finish_kernel(
+    scatter_hbm,
+    ret_hbm,
+    hidden_t_hbm,
+    out_grad_hbm,
+    router_grad_hbm,
+    token_grad,
+    down_grad,
+    router_grad,
+    scatter,
+    ret,
+    hidden_t,
+    out_grad,
+    token_buf,
+    down_buf,
+    load_sem,
+    store_sem,
+):
     ff = hidden_t.shape[0]
-    step = 128
+    parts = 4
+    step = ff // parts
+    pass_on = pltpu.make_async_copy(router_grad_hbm, router_grad, store_sem.at[2])
+    loads = [
+        pltpu.make_async_copy(out_grad_hbm, out_grad, load_sem.at[0]),
+        pltpu.make_async_copy(hidden_t_hbm, hidden_t, load_sem.at[1]),
+        pltpu.make_async_copy(ret_hbm, ret, load_sem.at[2]),
+        pltpu.make_async_copy(scatter_hbm, scatter, load_sem.at[3]),
+    ]
+    for load in loads:
+        load.start()
+    pass_on.start()
+    loads[0].wait()
+    loads[1].wait()
 
     def one(i, carry):
-        part = pl.ds(pl.multiple_of(i * step, step), step)
+        part = pl.ds(pl.multiple_of(i * step, 32), step)
         down_buf[part, :] = dot(hidden_t[part, :], out_grad[...]).astype(BF16)
-        pltpu.make_async_copy(down_buf.at[part, :], down_grad.at[part, :], sem.at[0]).start()
-        return carry
-
-    lax.fori_loop(0, ff // step, one, 0)
+        pltpu.make_async_copy(down_buf.at[part, :], down_grad.at[part, :], store_sem.at[0]).start()
+        return carry
+
+    lax.fori_loop(0, parts, one, 0)
+    loads[2].wait()
+    loads[3].wait()
     token_buf[...] = dot(scatter[...], ret[...]).astype(BF16)
-    store = pltpu.make_async_copy(token_buf, token_grad, sem.at[1])
+    store = pltpu.make_async_copy(token_buf, token_grad, store_sem.at[1])
     store.start()
-    pltpu.make_async_copy(down_buf, down_grad, sem.at[0]).wait()
+    pltpu.make_async_copy(down_buf, down_grad, store_sem.at[0]).wait()
     store.wait()
+    pass_on.wait()
 
 
 def local(n_node, n_chip, tokens, cotangent, chosen, group, router, w_gate, w_up, w_down):
@@ -428,9 +484,11 @@
             jax.ShapeDtypeStruct((dense, width), BF16),
             jax.ShapeDtypeStruct((1, width), F32),
         ],
-        in_specs=[vmem] * 3 + [hbm] * 5,
-        out_specs=[hbm] * 4 + [vmem],
+        in_specs=[hbm, vmem] + [hbm] * 6,
+        out_specs=[hbm] * 5,
         scratch_shapes=[
+            pltpu.VMEM((1, cap), jnp.int32),
+            pltpu.VMEM((1, width), BF16),
             pltpu.VMEM((row_count, 2 * width), BF16),
             pltpu.VMEM((width, ff), BF16),
             pltpu.VMEM((width, ff), BF16),
@@ -460,8 +518,9 @@
             pltpu.VMEM((packed, width), BF16),
             pltpu.VMEM((packed, width), BF16),
             pltpu.VMEM((row_count, packed), BF16),
+            pltpu.VMEM((1, width), F32),
+            dma((7,)),
             dma((5,)),
-            dma((4,)),
             dma((2,)),
             dma((2,)),
             dma((2 * STEPS,)),
@@ -474,7 +533,7 @@
             dma((STEPS,)),
         ],
         compiler_params=pltpu.CompilerParams(
-            collective_id=0, has_side_effects=True, vmem_limit_bytes=56 * 1024 * 1024
+            collective_id=0, has_side_effects=True, vmem_limit_bytes=58 * 1024 * 1024
         ),
         name="exchange",
     )(
@@ -487,22 +546,28 @@
         w_up[0],
         w_down[0],
     )
-    token_grad, down_grad = pl.pallas_call(
+    token_grad, down_grad, router_grad = pl.pallas_call(
         finish_kernel,
         out_shape=[
             jax.ShapeDtypeStruct((row_count, width), BF16),
             jax.ShapeDtypeStruct((ff, width), BF16),
+            jax.ShapeDtypeStruct((1, width), F32),
         ],
-        in_specs=[vmem] * 4,
-        out_specs=[hbm] * 2,
+        in_specs=[hbm] * 5,
+        out_specs=[hbm] * 3,
         scratch_shapes=[
+            pltpu.VMEM((row_count, packed), BF16),
+            pltpu.VMEM((packed, width), BF16),
+            pltpu.VMEM((ff, dense), BF16),
+            pltpu.VMEM((dense, width), BF16),
             pltpu.VMEM((row_count, width), BF16),
             pltpu.VMEM((ff, width), BF16),
-            dma((2,)),
+            dma((4,)),
+            dma((3,)),
         ],
-        compiler_params=pltpu.CompilerParams(vmem_limit_bytes=32 * 1024 * 1024),
+        compiler_params=pltpu.CompilerParams(vmem_limit_bytes=58 * 1024 * 1024),
         name="finish",
-    )(scatter, ret, hidden_t, out_grad)
+    )(scatter, ret, hidden_t, out_grad, router_grad)
     return token_grad, down_grad[None], router_grad
 
 

time: 98 us -> 77.6 us (0.79)
  Pallas kernels: 90.8 us -> 76.2 us
  local copies, waits for them, and re-layouts: 5.5 us -> 0 us
    pallas_call x1, Pallas kernels: 86 us -> 71.1 us  [local(): pl.pallas_call(functools.partial(exchange_kernel, n_node, n_chip), out_sh...]
    unnamed x9 -> x0, local copies, waits for them, and re-layouts: 5.5 us -> none
where the time goes in v2:
time: 77.6 us; the launch traced here: 77.5 us
  Pallas kernels  76.2 us (98%)
  between operations  1.29 us (2%)
    pallas_call x1, Pallas kernels, local(): pl.pallas_call(functools.partial(exchange_kernel, n_node, n_chip), out_sh...  71.1 us
    pallas_call x1, Pallas kernels, local(): pl.pallas_call(finish_kernel, out_shape=[jax.ShapeDtypeStruct((row_count,...  5.07 us

profile of v2, /device:TPU:1, one launch (start us, length us, event | category | flops | bytes accessed | tf_op | source)
XLA Modules:
  0.0 77.5 jit_solution(1943925660738639402)
XLA Ops:
  1.3 71.1 %exchange.1 = (bf16[128,2048]{1,0:T(8,128)(2,1)}, bf16[256,128]{1,0:T(8,128)(2,1)}, bf16[1408,256]{1,0:T(8,128)(2,1)}, bf16[256,2048]{1,0:T(8,128)(2,1)}, f32[1,2048]{1,0:T(1,128)}) custom-call(s32[1,256]{1,0:T(1,128)} %chosen_hbm.1, s32[1,1]{1,0:T(1,128)} %bitcast.5.group, bf16[1,2048]{1,0:T(2,128)(2,1)} %router_hbm.1, bf16[256,2048]{1,0:T(8,128)(2,1)} %tokens.1, ...), custom_call_target="tpu_custom_call" | custom-call | tf_op jit(solution)/shard_map/exchange/pallas_call | solution.py:478
  72.4 5.1 %finish.1 = (bf16[256,2048]{1,0:T(8,128)(2,1)}, bf16[1408,2048]{1,0:T(8,128)(2,1)}, f32[1,2048]{1,0:T(1,128)}) custom-call(bf16[256,128]{1,0:T(8,128)(2,1)} %get-tuple-element.11.scatter_hbm, bf16[128,2048]{1,0:T(8,128)(2,1)} %get-tuple-element.12.ret_hbm, bf16[1408,256]{1,0:T(8,128)(2,1)} %get-tuple-element.13.hidden_t_hbm, ...), custom_call_target="tpu_custom_call" | custom-call | tf_op jit(solution)/shard_map/finish/pallas_call | solution.py:549

commit v3 on v2

--- a/solution.py
+++ b/solution.py
@@ -10,6 +10,11 @@
 MESH = pl.DeviceIdType.MESH
 F32 = jnp.float32
 BF16 = jnp.bfloat16
+NODE_STEPS = (
+    (2, 2), (3, 2), (2, 3), (1, 2), (2, 1), (0, 2), (2, 0),
+    (3, 1), (1, 3), (3, 3), (1, 1), (0, 3), (3, 0), (0, 1), (1, 0),
+)
+CHIP_STEPS = (5, 4, 3, 2, 7, 6, 1)
 BLOCK = 16
 STEPS = 4
 LEAD = 2
@@ -35,11 +40,9 @@
     w_gate_hbm,
     w_up_hbm,
     w_down_hbm,
-    ret_out,
-    scatter_out,
-    hidden_t_out,
-    out_grad_out,
-    router_grad_out,
+    token_grad,
+    down_grad,
+    router_grad,
     chosen,
     router,
     both,
@@ -71,9 +74,7 @@
     back_stage,
     ret,
     scatter,
-    router_grad,
     load_sem,
-    store_sem,
     list_sem,
     pick_sem,
     a_send,
@@ -109,48 +110,40 @@
     for load in loads:
         load.start()
 
-    def node_peer(i):
-        return lax.rem(n + i, n_node)
+    def node_peer(step):
+        y, z = step
+        return lax.rem(n // 4 + y, 4) * 4 + lax.rem(lax.rem(n, 4) + z, 4)
 
     def chip_peer(i):
         return lax.rem(c + i, n_chip)
 
     barrier = pltpu.get_barrier_semaphore()
 
-    def greet_node(i, carry):
-        pl.semaphore_signal(barrier, inc=1, device_id=(node_peer(i), c), device_id_type=MESH)
-        return carry
-
-    def greet_chip(i, carry):
-        pl.semaphore_signal(barrier, inc=1, device_id=(n, chip_peer(i)), device_id_type=MESH)
-        return carry
-
-    lax.fori_loop(1, n_node, greet_node, 0)
-    lax.fori_loop(1, n_chip, greet_chip, 0)
+    for step in NODE_STEPS:
+        pl.semaphore_signal(barrier, inc=1, device_id=(node_peer(step), c), device_id_type=MESH)
+    for step in CHIP_STEPS:
+        pl.semaphore_signal(barrier, inc=1, device_id=(n, chip_peer(step)), device_id_type=MESH)
 
     for load in small_loads:
         load.wait()
     cap = chosen.shape[1]
-    slot_index = lax.broadcasted_iota(jnp.int32, (8, cap), 1)
-    live = jnp.right_shift(jnp.full((8, cap), cap, jnp.int32), jnp.broadcast_to(group[...], (8, cap)))
-    own_list = jnp.where(slot_index < live, jnp.broadcast_to(chosen[...], (8, cap)), -1)
+    slot_index = lax.broadcasted_iota(jnp.int32, (1, cap), 1)
+    live = jnp.right_shift(jnp.full((1, cap), cap, jnp.int32), jnp.broadcast_to(group[...], (1, cap)))
+    own_list = jnp.where(slot_index < live, chosen[...], -1)
     list_send[...] = own_list
-    lists[pl.ds(pl.multiple_of(n * 8, 8), 8), :] = own_list
+    lists[n] = own_list
 
     pl.semaphore_wait(barrier, n_node + n_chip - 2)
 
-    def send_list(i, carry):
+    for step in NODE_STEPS:
         pltpu.make_async_remote_copy(
             src_ref=list_send,
-            dst_ref=lists.at[pl.ds(pl.multiple_of(n * 8, 8), 8), :],
+            dst_ref=lists.at[n],
             send_sem=list_sem.at[0],
             recv_sem=list_sem.at[1],
-            device_id=(node_peer(i), c),
+            device_id=(node_peer(step), c),
             device_id_type=MESH,
         ).start()
-        return carry
-
-    lax.fori_loop(1, n_node, send_list, 0)
 
     pre_gate[...] = jnp.zeros_like(pre_gate)
     pre_up[...] = jnp.zeros_like(pre_up)
@@ -160,8 +153,7 @@
     def wait_bytes(ref, sem):
         pltpu.make_async_copy(ref, ref, sem).wait()
 
-    wait_bytes(lists.at[pl.ds(0, (n_node - 1) * 8), :], list_sem.at[0])
-    wait_bytes(lists.at[pl.ds(0, (n_node - 1) * 8), :], list_sem.at[1])
+    wait_bytes(lists.at[pl.ds(0, n_node - 1)], list_sem.at[1])
 
     source = lax.broadcasted_iota(jnp.int32, (8, 1), 0)
     lane_row = lax.broadcasted_iota(jnp.int32, (8, cap), 1)
@@ -169,7 +161,7 @@
     used = jnp.zeros((8, 1), jnp.int32)
     expand_parts, row_parts = [], []
     for e in range(n_node):
-        listed = lists[8 * e : 8 * e + 8, :]
+        listed = jnp.broadcast_to(lists[e], (8, cap))
         mine = jnp.right_shift(listed, 8) == n * n_chip + source
         local_row = jnp.bitwise_and(listed, 255)
         low = jnp.min(jnp.where(mine, local_row, 256), axis=1, keepdims=True)
@@ -191,8 +183,8 @@
     def block(i):
         return pl.ds(pl.multiple_of(i * BLOCK, BLOCK), BLOCK)
 
-    def send_pick(i, carry):
-        to = chip_peer(i)
+    for step in CHIP_STEPS:
+        to = chip_peer(step)
         pltpu.make_async_remote_copy(
             src_ref=pick_send.at[block(to), :],
             dst_ref=pick_mine.at[block(c), :],
@@ -201,21 +193,17 @@
             device_id=(n, to),
             device_id_type=MESH,
         ).start()
-        return carry
-
-    lax.fori_loop(1, n_chip, send_pick, 0)
     pick_mine[block(c), :] = pick_send[block(c), :]
     loads[0].wait()
     loads[1].wait()
-    wait_bytes(pick_mine.at[pl.ds(0, (n_chip - 1) * BLOCK), :], pick_sem.at[0])
     wait_bytes(pick_mine.at[pl.ds(0, (n_chip - 1) * BLOCK), :], pick_sem.at[1])
 
     def cols(s):
         return pl.ds(pl.multiple_of(s * chunk, chunk), chunk)
 
     def to_chips(src, dst, s, send_sem, recv_sem):
-        def one(i, carry):
-            to = chip_peer(i)
+        for step in CHIP_STEPS:
+            to = chip_peer(step)
             pltpu.make_async_remote_copy(
                 src_ref=src.at[block(to), cols(s)],
                 dst_ref=dst.at[block(c), cols(s)],
@@ -224,14 +212,11 @@
                 device_id=(n, to),
                 device_id_type=MESH,
             ).start()
-            return carry
-
-        lax.fori_loop(1, n_chip, one, 0)
         dst[block(c), cols(s)] = src[block(c), cols(s)]
 
     def to_nodes(src, dst, s, send_sem, recv_sem):
-        def one(i, carry):
-            to = node_peer(i)
+        for step in NODE_STEPS:
+            to = node_peer(step)
             pltpu.make_async_remote_copy(
                 src_ref=src.at[block(to), cols(s)],
                 dst_ref=dst.at[block(n), cols(s)],
@@ -240,9 +225,6 @@
                 device_id=(to, c),
                 device_id_type=MESH,
             ).start()
-            return carry
-
-        lax.fori_loop(1, n_node, one, 0)
         dst[block(n), cols(s)] = src[block(n), cols(s)]
 
     def chips_done(ref, s, sem):
@@ -289,8 +271,6 @@
     for s in range(LEAD):
         gather(s)
     scatter[...] = pick_mine[...].astype(F32).T.astype(BF16)
-    scatter_store = pltpu.make_async_copy(scatter, scatter_out, store_sem.at[0])
-    scatter_store.start()
 
     def phase(t, carry):
         @pl.when(t + LEAD < 2 * STEPS)
@@ -356,8 +336,6 @@
 
     lax.fori_loop(0, STEPS, return_phase, 0)
     hidden_t[...] = hidden[...].astype(F32).T.astype(BF16)
-    hidden_store = pltpu.make_async_copy(hidden_t, hidden_t_out, store_sem.at[1])
-    hidden_store.start()
 
     def scale(r, carry):
         part = pl.ds(pl.multiple_of(r * 16, 16), 16)
@@ -366,8 +344,12 @@
         return carry
 
     lax.fori_loop(0, dense // 16, scale, 0)
-    grad_store = pltpu.make_async_copy(out_grad, out_grad_out, store_sem.at[2])
-    grad_store.start()
+    def down_phase(r, carry):
+        part = pl.ds(pl.multiple_of(r * (ff // 4), 32), ff // 4)
+        down_grad[part, :] = dot(hidden_t[part, :], out_grad[...]).astype(BF16)
+        return carry
+
+    lax.fori_loop(0, 4, down_phase, 0)
 
     across = score_grad[...].T[:16, :]
     part0 = across.astype(BF16)
@@ -379,9 +361,6 @@
         value = dot(part0, x) + (dot(part1, x) + dot(part2, x))
         router_grad[:, s * chunk : (s + 1) * chunk] = value[:1, :]
 
-    router_store = pltpu.make_async_copy(router_grad, router_grad_out, store_sem.at[4])
-    router_store.start()
-
     def home_phase(s, carry):
         send_home(s)
         return carry
@@ -390,11 +369,12 @@
 
     def home(s, carry):
         chips_done(ret, s, ra_recv)
+        token_grad[:, cols(s)] = dot(scatter[...], ret[:, cols(s)]).astype(BF16)
         return carry
 
     lax.fori_loop(0, STEPS, home, 0)
-    ret_store = pltpu.make_async_copy(ret, ret_out, store_sem.at[3])
-    ret_store.start()
+    wait_bytes(lists.at[pl.ds(0, n_node - 1)], list_sem.at[0])
+    wait_bytes(pick_mine.at[pl.ds(0, (n_chip - 1) * BLOCK), :], pick_sem.at[0])
 
     def drain_out(s, carry):
         chips_done(stage_a, s, a_send)
@@ -408,62 +388,18 @@
 
     lax.fori_loop(0, 2 * STEPS, drain_out, 0)
     lax.fori_loop(0, STEPS, drain_back, 0)
-    scatter_store.wait()
-    hidden_store.wait()
-    grad_store.wait()
-    router_store.wait()
-    ret_store.wait()
-
-
-def finish_kernel(
-    scatter_hbm,
-    ret_hbm,
-    hidden_t_hbm,
-    out_grad_hbm,
-    router_grad_hbm,
-    token_grad,
-    down_grad,
-    router_grad,
-    scatter,
-    ret,
-    hidden_t,
-    out_grad,
-    token_buf,
-    down_buf,
-    load_sem,
-    store_sem,
-):
-    ff = hidden_t.shape[0]
-    parts = 4
-    step = ff // parts
-    pass_on = pltpu.make_async_copy(router_grad_hbm, router_grad, store_sem.at[2])
-    loads = [
-        pltpu.make_async_copy(out_grad_hbm, out_grad, load_sem.at[0]),
-        pltpu.make_async_copy(hidden_t_hbm, hidden_t, load_sem.at[1]),
-        pltpu.make_async_copy(ret_hbm, ret, load_sem.at[2]),
-        pltpu.make_async_copy(scatter_hbm, scatter, load_sem.at[3]),
+
+
+def finish_kernel(token_in, down_in, router_in, token_grad, down_grad, router_grad, sem):
+    stores = [
+        pltpu.make_async_copy(down_in, down_grad, sem.at[0]),
+        pltpu.make_async_copy(token_in, token_grad, sem.at[1]),
+        pltpu.make_async_copy(router_in, router_grad, sem.at[2]),
     ]
-    for load in loads:
-        load.start()
-    pass_on.start()
-    loads[0].wait()
-    loads[1].wait()
-
-    def one(i, carry):
-        part = pl.ds(pl.multiple_of(i * step, 32), step)
-        down_buf[part, :] = dot(hidden_t[part, :], out_grad[...]).astype(BF16)
-        pltpu.make_async_copy(down_buf.at[part, :], down_grad.at[part, :], store_sem.at[0]).start()
-        return carry
-
-    lax.fori_loop(0, parts, one, 0)
-    loads[2].wait()
-    loads[3].wait()
-    token_buf[...] = dot(scatter[...], ret[...]).astype(BF16)
-    store = pltpu.make_async_copy(token_buf, token_grad, store_sem.at[1])
-    store.start()
-    pltpu.make_async_copy(down_buf, down_grad, store_sem.at[0]).wait()
-    store.wait()
-    pass_on.wait()
+    for store in stores:
+        store.start()
+    for store in stores:
+        store.wait()
 
 
 def local(n_node, n_chip, tokens, cotangent, chosen, group, router, w_gate, w_up, w_down):
@@ -475,17 +411,15 @@
     vmem = pl.BlockSpec(memory_space=pltpu.VMEM)
     hbm = pl.BlockSpec(memory_space=pl.ANY)
     dma = pltpu.SemaphoreType.DMA
-    ret, scatter, hidden_t, out_grad, router_grad = pl.pallas_call(
+    results = pl.pallas_call(
         functools.partial(exchange_kernel, n_node, n_chip),
         out_shape=[
-            jax.ShapeDtypeStruct((packed, width), BF16),
-            jax.ShapeDtypeStruct((row_count, packed), BF16),
-            jax.ShapeDtypeStruct((ff, dense), BF16),
-            jax.ShapeDtypeStruct((dense, width), BF16),
-            jax.ShapeDtypeStruct((1, width), F32),
+            pltpu.VMEM((row_count, width), BF16),
+            pltpu.VMEM((ff, width), BF16),
+            pltpu.VMEM((1, width), F32),
         ],
         in_specs=[hbm, vmem] + [hbm] * 6,
-        out_specs=[hbm] * 5,
+        out_specs=[vmem] * 3,
         scratch_shapes=[
             pltpu.VMEM((1, cap), jnp.int32),
             pltpu.VMEM((1, width), BF16),
@@ -493,8 +427,8 @@
             pltpu.VMEM((width, ff), BF16),
             pltpu.VMEM((width, ff), BF16),
             pltpu.VMEM((ff, width), BF16),
-            pltpu.VMEM((8, cap), jnp.int32),
-            pltpu.VMEM((8 * n_node, cap), jnp.int32),
+            pltpu.VMEM((1, cap), jnp.int32),
+            pltpu.VMEM((n_node, 1, cap), jnp.int32),
             pltpu.VMEM((dense, packed), BF16),
             pltpu.VMEM((packed, dense), BF16),
             pltpu.VMEM((packed, row_count), BF16),
@@ -518,9 +452,7 @@
             pltpu.VMEM((packed, width), BF16),
             pltpu.VMEM((packed, width), BF16),
             pltpu.VMEM((row_count, packed), BF16),
-            pltpu.VMEM((1, width), F32),
             dma((7,)),
-            dma((5,)),
             dma((2,)),
             dma((2,)),
             dma((2 * STEPS,)),
@@ -533,7 +465,7 @@
             dma((STEPS,)),
         ],
         compiler_params=pltpu.CompilerParams(
-            collective_id=0, has_side_effects=True, vmem_limit_bytes=58 * 1024 * 1024
+            collective_id=0, has_side_effects=True, vmem_limit_bytes=48 * 1024 * 1024
         ),
         name="exchange",
     )(
@@ -553,21 +485,12 @@
             jax.ShapeDtypeStruct((ff, width), BF16),
             jax.ShapeDtypeStruct((1, width), F32),
         ],
-        in_specs=[hbm] * 5,
+        in_specs=[vmem] * 3,
         out_specs=[hbm] * 3,
-        scratch_shapes=[
-            pltpu.VMEM((row_count, packed), BF16),
-            pltpu.VMEM((packed, width), BF16),
-            pltpu.VMEM((ff, dense), BF16),
-            pltpu.VMEM((dense, width), BF16),
-            pltpu.VMEM((row_count, width), BF16),
-            pltpu.VMEM((ff, width), BF16),
-            dma((4,)),
-            dma((3,)),
-        ],
-        compiler_params=pltpu.CompilerParams(vmem_limit_bytes=58 * 1024 * 1024),
+        scratch_shapes=[dma((3,))],
+        compiler_params=pltpu.CompilerParams(vmem_limit_bytes=16 * 1024 * 1024),
         name="finish",
-    )(scatter, ret, hidden_t, out_grad, router_grad)
+    )(*results)
     return token_grad, down_grad[None], router_grad
 
 

time: 77.6 us -> 71.1 us (0.916)
  Pallas kernels: 76.2 us -> 69.7 us
    pallas_call x1, Pallas kernels: 71.1 us -> 66.8 us  [local(): pl.pallas_call(functools.partial(exchange_kernel, n_node, n_chip), out_sh...]
    pallas_call x1, Pallas kernels: 5.07 us -> 2.9 us  [local(): pl.pallas_call(finish_kernel, out_shape=[jax.ShapeDtypeStruct((row_count,...]
where the time goes in v3:
time: 71.1 us; the launch traced here: 71 us
  Pallas kernels  69.7 us (98%)
  between operations  1.29 us (2%)
    pallas_call x1, Pallas kernels, local(): pl.pallas_call(functools.partial(exchange_kernel, n_node, n_chip), out_sh...  66.8 us
    pallas_call x1, Pallas kernels, local(): pl.pallas_call(finish_kernel, out_shape=[jax.ShapeDtypeStruct((row_count,...  2.9 us

profile of v3, /device:TPU:1, one launch (start us, length us, event | category | flops | bytes accessed | tf_op | source)
XLA Modules:
  0.0 71.0 jit_solution(13903239255324538551)
XLA Ops:
  1.3 66.8 %exchange.1 = (bf16[256,2048]{1,0:T(8,128)(2,1)S(1)}, bf16[1408,2048]{1,0:T(8,128)(2,1)S(1)}, f32[1,2048]{1,0:T(1,128)S(1)}) custom-call(s32[1,256]{1,0:T(1,128)} %chosen_hbm.1, s32[1,1]{1,0:T(1,128)} %bitcast.5.group, bf16[1,2048]{1,0:T(2,128)(2,1)} %router_hbm.1, bf16[256,2048]{1,0:T(8,128)(2,1)} %tokens.1, bf16[256,2048]{1,0:T(8,128)(2,1)} %cotangent.1, ...), custom_call_target="tpu_custom_call" | custom-call | tf_op jit(solution)/shard_map/exchange/pallas_call | solution.py:414
  68.1 2.9 %finish.1 = (bf16[256,2048]{1,0:T(8,128)(2,1)}, bf16[1408,2048]{1,0:T(8,128)(2,1)}, f32[1,2048]{1,0:T(1,128)}) custom-call(bf16[256,2048]{1,0:T(8,128)(2,1)S(1)} %get-tuple-element.9.token_in, bf16[1408,2048]{1,0:T(8,128)(2,1)S(1)} %get-tuple-element.10.down_in, f32[1,2048]{1,0:T(1,128)S(1)} %get-tuple-element.11.router_in), custom_call_target="tpu_custom_call" | custom-call | tf_op jit(solution)/shard_map/finish/pallas_call | solution.py:481

commit v4 on v3

--- a/solution.py
+++ b/solution.py
@@ -17,8 +17,9 @@
 CHIP_STEPS = (5, 4, 3, 2, 7, 6, 1)
 BLOCK = 16
 STEPS = 4
+FIRST = 2
 LEAD = 2
-LAG = 3
+LAG = 4
 
 
 def dot(a, b):
@@ -74,9 +75,25 @@
     back_stage,
     ret,
     scatter,
+    perm,
+    perm_t,
+    full_send,
+    full_mine,
+    full_pick,
+    full_scatter,
+    first_mid,
+    first_turn,
+    first_got,
+    last_turn,
+    last_mid,
+    last_stage,
+    last_got,
     load_sem,
     list_sem,
     pick_sem,
+    full_sem,
+    first_sem,
+    last_sem,
     a_send,
     a_recv,
     b_send,
@@ -149,6 +166,14 @@
     pre_up[...] = jnp.zeros_like(pre_up)
     raw[...] = jnp.zeros_like(raw)
     score[...] = jnp.zeros_like(score)
+
+    def order(axis):
+        i = lax.broadcasted_iota(jnp.int32, (dense, dense), axis)
+        by_node = jnp.bitwise_and(i, 7) * 32 + jnp.bitwise_and(jnp.right_shift(i, 3), 1) * 16 + jnp.right_shift(i, 4)
+        return jnp.where(by_node == lax.broadcasted_iota(jnp.int32, (dense, dense), 1 - axis), 1.0, 0.0)
+
+    perm[...] = order(0).astype(BF16)
+    perm_t[...] = order(1).astype(BF16)
 
     def wait_bytes(ref, sem):
         pltpu.make_async_copy(ref, ref, sem).wait()
@@ -172,17 +197,38 @@
         expand_parts.append(jnp.where(lane_slot == first, 1.0, 0.0))
         expand_parts.append(jnp.where(lane_slot == second, 1.0, 0.0))
         row_parts.append(jnp.where(lane_row == low, 1.0, 0.0))
-        row_parts.append(jnp.where(lane_row == high, 1.0, 0.0))
+        row_parts.append(jnp.where(lane_row == jnp.where(high > low, high, -1), 1.0, 0.0))
         used = used + jnp.where(high >= 0, 1, 0)
     expand_f32 = jnp.concatenate(expand_parts, axis=0)
     expand[...] = expand_f32.astype(BF16)
     compact[...] = expand_f32.T.astype(BF16)
     row_hot = jnp.concatenate(row_parts, axis=0).astype(BF16)
-    pick_send[...] = dot(compact[...], row_hot).astype(BF16)
+    full_send[...] = dot(perm_t[...], row_hot).astype(BF16)
 
     def block(i):
         return pl.ds(pl.multiple_of(i * BLOCK, BLOCK), BLOCK)
 
+    def wide(i):
+        return pl.ds(pl.multiple_of(i * 2 * BLOCK, 2 * BLOCK), 2 * BLOCK)
+
+    def turn_to_chips(src, dst, sem, at=slice(None)):
+        for step in CHIP_STEPS:
+            to = chip_peer(step)
+            pltpu.make_async_remote_copy(
+                src_ref=src.at[wide(to), at],
+                dst_ref=dst.at[wide(c), at],
+                send_sem=sem.at[0],
+                recv_sem=sem.at[1],
+                device_id=(n, to),
+                device_id_type=MESH,
+            ).start()
+        dst[wide(c), at] = src[wide(c), at]
+
+    def turn_done(ref, sem, at=slice(None)):
+        wait_bytes(ref.at[pl.ds(0, dense - 2 * BLOCK), at], sem)
+
+    turn_to_chips(full_send, full_mine, full_sem)
+    pick_send[...] = dot(compact[...], row_hot).astype(BF16)
     for step in CHIP_STEPS:
         to = chip_peer(step)
         pltpu.make_async_remote_copy(
@@ -194,9 +240,6 @@
             device_id_type=MESH,
         ).start()
     pick_mine[block(c), :] = pick_send[block(c), :]
-    loads[0].wait()
-    loads[1].wait()
-    wait_bytes(pick_mine.at[pl.ds(0, (n_chip - 1) * BLOCK), :], pick_sem.at[1])
 
     def cols(s):
         return pl.ds(pl.multiple_of(s * chunk, chunk), chunk)
@@ -214,18 +257,20 @@
             ).start()
         dst[block(c), cols(s)] = src[block(c), cols(s)]
 
-    def to_nodes(src, dst, s, send_sem, recv_sem):
+    def to_nodes(src, dst, s, send_sem, recv_sem, src_cols=None, dst_cols=None):
+        src_cols = cols(s) if src_cols is None else src_cols
+        dst_cols = cols(s) if dst_cols is None else dst_cols
         for step in NODE_STEPS:
             to = node_peer(step)
             pltpu.make_async_remote_copy(
-                src_ref=src.at[block(to), cols(s)],
-                dst_ref=dst.at[block(n), cols(s)],
+                src_ref=src.at[block(to), src_cols],
+                dst_ref=dst.at[block(n), dst_cols],
                 send_sem=send_sem.at[s],
                 recv_sem=recv_sem.at[s],
                 device_id=(to, c),
                 device_id_type=MESH,
             ).start()
-        dst[block(n), cols(s)] = src[block(n), cols(s)]
+        dst[block(n), dst_cols] = src[block(n), src_cols]
 
     def chips_done(ref, s, sem):
         wait_bytes(ref.at[pl.ds(0, packed - BLOCK), cols(s)], sem.at[s])
@@ -243,7 +288,6 @@
         to_nodes(stage_b, rows, s, b_send, b_recv)
 
     def up_step(s):
-        nodes_done(rows, s, b_recv)
         x = rows[:, cols(s)]
         pre_gate[...] += dot(x, w_gate[cols(s), :])
         pre_up[...] += dot(x, w_up[cols(s), :])
@@ -268,9 +312,23 @@
             pre_up[part, lanes] = s * act
         return carry
 
-    for s in range(LEAD):
+    whole = pl.ds(0, chunk)
+    turn_done(full_mine, full_sem.at[1])
+    full_pick[...] = dot(perm[...], full_mine[...]).astype(BF16)
+    loads[0].wait()
+
+    def first_phase(s, carry):
+        stage_b[:, cols(s)] = dot(full_pick[...], both[:, cols(s)]).astype(BF16)
+        to_nodes(stage_b, first_mid, s, b_send, b_recv)
+        return carry
+
+    lax.fori_loop(0, FIRST, first_phase, 0)
+    loads[1].wait()
+    wait_bytes(pick_mine.at[pl.ds(0, (n_chip - 1) * BLOCK), :], pick_sem.at[1])
+    for s in range(FIRST, FIRST + LEAD):
         gather(s)
     scatter[...] = pick_mine[...].astype(F32).T.astype(BF16)
+    full_scatter[...] = full_pick[...].astype(F32).T.astype(BF16)
 
     def phase(t, carry):
         @pl.when(t + LEAD < 2 * STEPS)
@@ -281,11 +339,28 @@
         def _():
             forward(t)
 
+        @pl.when(t < 2 * FIRST)
+        def _():
+            f = t - FIRST
+            nodes_done(first_mid, f, b_recv)
+            first_turn[:, cols(f)] = dot(perm_t[...], first_mid[:, cols(f)]).astype(BF16)
+            turn_to_chips(first_turn, first_got, first_sem.at[f], cols(f))
+
         @pl.when(t == LAG)
         def _():
             loads[2].wait()
             loads[3].wait()
 
+        @pl.when((t >= LAG) & (t < FIRST + LAG))
+        def _():
+            f = t - LAG
+            turn_done(first_got, first_sem.at[f, 1], cols(f))
+            rows[:, cols(f)] = dot(perm[...], first_got[:, cols(f)]).astype(BF16)
+
+        @pl.when((t >= FIRST + LAG) & (t < STEPS + LAG))
+        def _():
+            nodes_done(rows, t - LAG, b_recv)
+
         @pl.when((t >= LAG) & (t < STEPS + LAG))
         def _():
             up_step(t - LAG)
@@ -301,7 +376,7 @@
 
         return carry
 
-    lax.fori_loop(0, 2 * STEPS + LAG, phase, 0)
+    lax.fori_loop(FIRST, 2 * STEPS + LAG, phase, 0)
 
     def from_dy(r, carry):
         part = pl.ds(pl.multiple_of(r * 64, 64), 64)
@@ -318,11 +393,14 @@
 
     lax.fori_loop(0, dense // 64, from_dy, 0)
 
-    def send_back(s):
+    def pick_chunk(s):
         value = dot_nt(gate_grad[...], w_gate[cols(s), :])
         value = value + dot_nt(up_grad[...], w_up[cols(s), :])
         value = value + score_grad[:, :1] * router[:, cols(s)].astype(F32)
         back[:, cols(s)] = value.astype(BF16)
+
+    def send_back(s):
+        pick_chunk(s)
         to_nodes(back, back_mid, s, rb_send, rb_recv)
 
     def send_home(s):
@@ -334,7 +412,12 @@
         send_back(s)
         return carry
 
-    lax.fori_loop(0, STEPS, return_phase, 0)
+    final = STEPS - 1
+    send_back(0)
+    pick_chunk(final)
+    last_turn[...] = dot(perm_t[...], back[:, cols(final)]).astype(BF16)
+    turn_to_chips(last_turn, last_mid, last_sem)
+    lax.fori_loop(1, final, return_phase, 0)
     hidden_t[...] = hidden[...].astype(F32).T.astype(BF16)
 
     def scale(r, carry):
@@ -350,6 +433,10 @@
         return carry
 
     lax.fori_loop(0, 4, down_phase, 0)
+
+    turn_done(last_mid, last_sem.at[1])
+    last_stage[...] = dot(perm[...], last_mid[...]).astype(BF16)
+    to_nodes(last_stage, last_got, final, rb_send, rb_recv, whole, whole)
 
     across = score_grad[...].T[:16, :]
     part0 = across.astype(BF16)
@@ -365,16 +452,26 @@
         send_home(s)
         return carry
 
-    lax.fori_loop(0, STEPS, home_phase, 0)
+    lax.fori_loop(0, final, home_phase, 0)
 
     def home(s, carry):
         chips_done(ret, s, ra_recv)
         token_grad[:, cols(s)] = dot(scatter[...], ret[:, cols(s)]).astype(BF16)
         return carry
 
-    lax.fori_loop(0, STEPS, home, 0)
+    lax.fori_loop(0, final, home, 0)
+    wait_bytes(last_got.at[pl.ds(0, dense - BLOCK), :], rb_recv.at[final])
+    token_grad[:, cols(final)] = dot(full_scatter[...], last_got[...]).astype(BF16)
     wait_bytes(lists.at[pl.ds(0, n_node - 1)], list_sem.at[0])
     wait_bytes(pick_mine.at[pl.ds(0, (n_chip - 1) * BLOCK), :], pick_sem.at[0])
+
+    turn_done(full_send, full_sem.at[0])
+    for f in range(FIRST):
+        turn_done(first_turn, first_sem.at[f, 0], cols(f))
+    turn_done(last_turn, last_sem.at[0])
+    wait_bytes(last_stage.at[pl.ds(0, dense - BLOCK), :], rb_send.at[final])
+    for f in range(FIRST):
+        nodes_done(stage_b, f, b_send)
 
     def drain_out(s, carry):
         chips_done(stage_a, s, a_send)
@@ -386,8 +483,8 @@
         chips_done(back_stage, s, ra_send)
         return carry
 
-    lax.fori_loop(0, 2 * STEPS, drain_out, 0)
-    lax.fori_loop(0, STEPS, drain_back, 0)
+    lax.fori_loop(FIRST, 2 * STEPS, drain_out, 0)
+    lax.fori_loop(0, final, drain_back, 0)
 
 
 def finish_kernel(token_in, down_in, router_in, token_grad, down_grad, router_grad, sem):
@@ -452,8 +549,24 @@
             pltpu.VMEM((packed, width), BF16),
             pltpu.VMEM((packed, width), BF16),
             pltpu.VMEM((row_count, packed), BF16),
+            pltpu.VMEM((dense, dense), BF16),
+            pltpu.VMEM((dense, dense), BF16),
+            pltpu.VMEM((dense, row_count), BF16),
+            pltpu.VMEM((dense, row_count), BF16),
+            pltpu.VMEM((dense, row_count), BF16),
+            pltpu.VMEM((row_count, dense), BF16),
+            pltpu.VMEM((dense, FIRST * width // STEPS), BF16),
+            pltpu.VMEM((dense, FIRST * width // STEPS), BF16),
+            pltpu.VMEM((dense, FIRST * width // STEPS), BF16),
+            pltpu.VMEM((dense, width // STEPS), BF16),
+            pltpu.VMEM((dense, width // STEPS), BF16),
+            pltpu.VMEM((dense, width // STEPS), BF16),
+            pltpu.VMEM((dense, width // STEPS), BF16),
             dma((7,)),
             dma((2,)),
+            dma((2,)),
+            dma((2,)),
+            dma((FIRST, 2)),
             dma((2,)),
             dma((2 * STEPS,)),
             dma((2 * STEPS,)),

time: 71.1 us -> 67.1 us (0.944)
  Pallas kernels: 69.7 us -> 65.7 us
    pallas_call x1, Pallas kernels: 66.8 us -> 62.8 us  [local(): pl.pallas_call(functools.partial(exchange_kernel, n_node, n_chip), out_sh...]
where the time goes in v4:
time: 67.1 us; the launch traced here: 67 us
  Pallas kernels  65.7 us (98%)
  between operations  1.29 us (2%)
    pallas_call x1, Pallas kernels, local(): pl.pallas_call(functools.partial(exchange_kernel, n_node, n_chip), out_sh...  62.8 us
    pallas_call x1, Pallas kernels, local(): pl.pallas_call(finish_kernel, out_shape=[jax.ShapeDtypeStruct((row_count,...  2.9 us

profile of v4, /device:TPU:1, one launch (start us, length us, event | category | flops | bytes accessed | tf_op | source)
XLA Modules:
  0.0 67.0 jit_solution(7831310185900070006)
XLA Ops:
  1.3 62.8 %exchange.1 = (bf16[256,2048]{1,0:T(8,128)(2,1)S(1)}, bf16[1408,2048]{1,0:T(8,128)(2,1)S(1)}, f32[1,2048]{1,0:T(1,128)S(1)}) custom-call(s32[1,256]{1,0:T(1,128)} %chosen_hbm.1, s32[1,1]{1,0:T(1,128)} %bitcast.5.group, bf16[1,2048]{1,0:T(2,128)(2,1)} %router_hbm.1, bf16[256,2048]{1,0:T(8,128)(2,1)} %tokens.1, bf16[256,2048]{1,0:T(8,128)(2,1)} %cotangent.1, ...), custom_call_target="tpu_custom_call" | custom-call | tf_op jit(solution)/shard_map/exchange/pallas_call | solution.py:511
  64.1 2.9 %finish.1 = (bf16[256,2048]{1,0:T(8,128)(2,1)}, bf16[1408,2048]{1,0:T(8,128)(2,1)}, f32[1,2048]{1,0:T(1,128)}) custom-call(bf16[256,2048]{1,0:T(8,128)(2,1)S(1)} %get-tuple-element.9.token_in, bf16[1408,2048]{1,0:T(8,128)(2,1)S(1)} %get-tuple-element.10.down_in, f32[1,2048]{1,0:T(1,128)S(1)} %get-tuple-element.11.router_in), custom_call_target="tpu_custom_call" | custom-call | tf_op jit(solution)/shard_map/finish/pallas_call | solution.py:594

commit v5 on v4

--- a/solution.py
+++ b/solution.py
@@ -18,6 +18,7 @@
 BLOCK = 16
 STEPS = 4
 FIRST = 2
+FINAL = 1
 LEAD = 2
 LAG = 4
 
@@ -184,7 +185,7 @@
     lane_row = lax.broadcasted_iota(jnp.int32, (8, cap), 1)
     lane_slot = lax.broadcasted_iota(jnp.int32, (8, packed), 1)
     used = jnp.zeros((8, 1), jnp.int32)
-    expand_parts, row_parts = [], []
+    expand_parts, row_parts, number_parts = [], [], []
     for e in range(n_node):
         listed = jnp.broadcast_to(lists[e], (8, cap))
         mine = jnp.right_shift(listed, 8) == n * n_chip + source
@@ -197,13 +198,12 @@
         expand_parts.append(jnp.where(lane_slot == first, 1.0, 0.0))
         expand_parts.append(jnp.where(lane_slot == second, 1.0, 0.0))
         row_parts.append(jnp.where(lane_row == low, 1.0, 0.0))
-        row_parts.append(jnp.where(lane_row == jnp.where(high > low, high, -1), 1.0, 0.0))
+        row_parts.append(jnp.where(lane_row == high, 1.0, 0.0))
+        number_parts.append(jnp.broadcast_to(jnp.where(high >= 0, low, -1), (8, 128)))
+        number_parts.append(jnp.broadcast_to(jnp.where(high > low, high, -1), (8, 128)))
         used = used + jnp.where(high >= 0, 1, 0)
-    expand_f32 = jnp.concatenate(expand_parts, axis=0)
-    expand[...] = expand_f32.astype(BF16)
-    compact[...] = expand_f32.T.astype(BF16)
-    row_hot = jnp.concatenate(row_parts, axis=0).astype(BF16)
-    full_send[...] = dot(perm_t[...], row_hot).astype(BF16)
+    numbers = jnp.concatenate(number_parts, axis=0).astype(F32).astype(BF16)
+    full_send[...] = dot(perm_t[...], numbers).astype(BF16)
 
     def block(i):
         return pl.ds(pl.multiple_of(i * BLOCK, BLOCK), BLOCK)
@@ -228,6 +228,10 @@
         wait_bytes(ref.at[pl.ds(0, dense - 2 * BLOCK), at], sem)
 
     turn_to_chips(full_send, full_mine, full_sem)
+    expand_f32 = jnp.concatenate(expand_parts, axis=0)
+    expand[...] = expand_f32.astype(BF16)
+    compact[...] = expand_f32.T.astype(BF16)
+    row_hot = jnp.concatenate(row_parts, axis=0).astype(BF16)
     pick_send[...] = dot(compact[...], row_hot).astype(BF16)
     for step in CHIP_STEPS:
         to = chip_peer(step)
@@ -312,9 +316,11 @@
             pre_up[part, lanes] = s * act
         return carry
 
-    whole = pl.ds(0, chunk)
     turn_done(full_mine, full_sem.at[1])
-    full_pick[...] = dot(perm[...], full_mine[...]).astype(BF16)
+    wanted = dot(perm[...], full_mine[...])
+    lane = lax.broadcasted_iota(jnp.int32, (dense, 128), 1).astype(F32)
+    for h in range(full_pick.shape[1] // 128):
+        full_pick[:, 128 * h : 128 * (h + 1)] = jnp.where(wanted == lane + 128.0 * h, 1.0, 0.0).astype(BF16)
     loads[0].wait()
 
     def first_phase(s, carry):
@@ -412,12 +418,23 @@
         send_back(s)
         return carry
 
-    final = STEPS - 1
-    send_back(0)
-    pick_chunk(final)
-    last_turn[...] = dot(perm_t[...], back[:, cols(final)]).astype(BF16)
-    turn_to_chips(last_turn, last_mid, last_sem)
-    lax.fori_loop(1, final, return_phase, 0)
+    final = STEPS - FINAL
+
+    def final_turn(f, carry):
+        pick_chunk(final + f)
+        last_turn[:, cols(f)] = dot(perm_t[...], back[:, cols(final + f)]).astype(BF16)
+        turn_to_chips(last_turn, last_mid, last_sem.at[f], cols(f))
+        return carry
+
+    def final_phase(f, carry):
+        turn_done(last_mid, last_sem.at[f, 1], cols(f))
+        last_stage[:, cols(f)] = dot(perm[...], last_mid[:, cols(f)]).astype(BF16)
+        to_nodes(last_stage, last_got, final + f, rb_send, rb_recv, cols(f), cols(f))
+        return carry
+
+    lax.fori_loop(0, FINAL, return_phase, 0)
+    lax.fori_loop(0, FINAL, final_turn, 0)
+    lax.fori_loop(FINAL, final, return_phase, 0)
     hidden_t[...] = hidden[...].astype(F32).T.astype(BF16)
 
     def scale(r, carry):
@@ -434,9 +451,7 @@
 
     lax.fori_loop(0, 4, down_phase, 0)
 
-    turn_done(last_mid, last_sem.at[1])
-    last_stage[...] = dot(perm[...], last_mid[...]).astype(BF16)
-    to_nodes(last_stage, last_got, final, rb_send, rb_recv, whole, whole)
+    lax.fori_loop(0, FINAL, final_phase, 0)
 
     across = score_grad[...].T[:16, :]
     part0 = across.astype(BF16)
@@ -460,16 +475,22 @@
         return carry
 
     lax.fori_loop(0, final, home, 0)
-    wait_bytes(last_got.at[pl.ds(0, dense - BLOCK), :], rb_recv.at[final])
-    token_grad[:, cols(final)] = dot(full_scatter[...], last_got[...]).astype(BF16)
+
+    def final_home(f, carry):
+        wait_bytes(last_got.at[pl.ds(0, dense - BLOCK), cols(f)], rb_recv.at[final + f])
+        token_grad[:, cols(final + f)] = dot(full_scatter[...], last_got[:, cols(f)]).astype(BF16)
+        return carry
+
+    lax.fori_loop(0, FINAL, final_home, 0)
     wait_bytes(lists.at[pl.ds(0, n_node - 1)], list_sem.at[0])
     wait_bytes(pick_mine.at[pl.ds(0, (n_chip - 1) * BLOCK), :], pick_sem.at[0])
 
     turn_done(full_send, full_sem.at[0])
     for f in range(FIRST):
         turn_done(first_turn, first_sem.at[f, 0], cols(f))
-    turn_done(last_turn, last_sem.at[0])
-    wait_bytes(last_stage.at[pl.ds(0, dense - BLOCK), :], rb_send.at[final])
+    for f in range(FINAL):
+        turn_done(last_turn, last_sem.at[f, 0], cols(f))
+        wait_bytes(last_stage.at[pl.ds(0, dense - BLOCK), cols(f)], rb_send.at[final + f])
     for f in range(FIRST):
         nodes_done(stage_b, f, b_send)
 
@@ -551,23 +572,23 @@
             pltpu.VMEM((row_count, packed), BF16),
             pltpu.VMEM((dense, dense), BF16),
             pltpu.VMEM((dense, dense), BF16),
-            pltpu.VMEM((dense, row_count), BF16),
-            pltpu.VMEM((dense, row_count), BF16),
+            pltpu.VMEM((dense, 128), BF16),
+            pltpu.VMEM((dense, 128), BF16),
             pltpu.VMEM((dense, row_count), BF16),
             pltpu.VMEM((row_count, dense), BF16),
             pltpu.VMEM((dense, FIRST * width // STEPS), BF16),
             pltpu.VMEM((dense, FIRST * width // STEPS), BF16),
             pltpu.VMEM((dense, FIRST * width // STEPS), BF16),
-            pltpu.VMEM((dense, width // STEPS), BF16),
-            pltpu.VMEM((dense, width // STEPS), BF16),
-            pltpu.VMEM((dense, width // STEPS), BF16),
-            pltpu.VMEM((dense, width // STEPS), BF16),
+            pltpu.VMEM((dense, FINAL * width // STEPS), BF16),
+            pltpu.VMEM((dense, FINAL * width // STEPS), BF16),
+            pltpu.VMEM((dense, FINAL * width // STEPS), BF16),
+            pltpu.VMEM((dense, FINAL * width // STEPS), BF16),
             dma((7,)),
             dma((2,)),
             dma((2,)),
             dma((2,)),
             dma((FIRST, 2)),
-            dma((2,)),
+            dma((FINAL, 2)),
             dma((2 * STEPS,)),
             dma((2 * STEPS,)),
             dma((2 * STEPS,)),

time: 67.1 us -> 66.9 us (level)
  no operation moved by 1% of the time
where the time goes in v5:
time: 66.9 us; the launch traced here: 66.7 us
  Pallas kernels  65.5 us (98%)
  between operations  1.29 us (2%)
    pallas_call x1, Pallas kernels, local(): pl.pallas_call(functools.partial(exchange_kernel, n_node, n_chip), out_sh...  62.6 us
    pallas_call x1, Pallas kernels, local(): pl.pallas_call(finish_kernel, out_shape=[jax.ShapeDtypeStruct((row_count,...  2.9 us

profile of v5, /device:TPU:1, one launch (start us, length us, event | category | flops | bytes accessed | tf_op | source)
XLA Modules:
  0.0 66.7 jit_solution(16003699908453193873)
XLA Ops:
  1.3 62.6 %exchange.1 = (bf16[256,2048]{1,0:T(8,128)(2,1)S(1)}, bf16[1408,2048]{1,0:T(8,128)(2,1)S(1)}, f32[1,2048]{1,0:T(1,128)S(1)}) custom-call(s32[1,256]{1,0:T(1,128)} %chosen_hbm.1, s32[1,1]{1,0:T(1,128)} %bitcast.5.group, bf16[1,2048]{1,0:T(2,128)(2,1)} %router_hbm.1, bf16[256,2048]{1,0:T(8,128)(2,1)} %tokens.1, bf16[256,2048]{1,0:T(8,128)(2,1)} %cotangent.1, ...), custom_call_target="tpu_custom_call" | custom-call | tf_op jit(solution)/shard_map/exchange/pallas_call | solution.py:532
  63.8 2.9 %finish.1 = (bf16[256,2048]{1,0:T(8,128)(2,1)}, bf16[1408,2048]{1,0:T(8,128)(2,1)}, f32[1,2048]{1,0:T(1,128)}) custom-call(bf16[256,2048]{1,0:T(8,128)(2,1)S(1)} %get-tuple-element.9.token_in, bf16[1408,2048]{1,0:T(8,128)(2,1)S(1)} %get-tuple-element.10.down_in, f32[1,2048]{1,0:T(1,128)S(1)} %get-tuple-element.11.router_in), custom_call_target="tpu_custom_call" | custom-call | tf_op jit(solution)/shard_map/finish/pallas_call | solution.py:615
